TPU v7x, 512 devices: a whole 4x4x16 slice. The times are simulated.
512 devices in a mesh: row: 16 (over z_lo, y), col: 32 (over x, z_hi, core).
Axes of the slice: x: 4, y: 4, z: 16 (z_hi: 4, z_lo: 4; z = z_hi * 4 + z_lo), core: 2. Of those that a mesh axis runs over, the one named last changes fastest.
Arguments:
- hamiltonian: bfloat16 [2048, 65536], P('row', 'col'), may hold values from -0.125 to 0.125
- z_panel: bfloat16 [65536, 4096], P('row', 'col'), may hold values from -6 to 6
- z_slab: bfloat16 [2048, 4096], P('row', 'col'), may hold values from -0.125 to 0.125
- mask_h: int32 [32, 1024], P('row', 'col'), may hold values 0 or 1
- mask_panel: int32 [1024, 64], P('row', 'col'), may hold values 0 or 1
- mask_slab: int32 [32, 64], P('row', 'col'), may hold values 0 or 1
- section_blocks: int32 [2, 16], replicated, may hold values from 0 to 1023, as said below
Outputs:
- k_transposed: bfloat16 [4096, 4096], P('row', 'col')
Inputs may be any that keep to these rules, and one draw needn't show every extreme that they name: `section_blocks`: each row holds 16 distinct block indices that all lie in one aligned group of 32 consecutive inner blocks; different rows lie in different groups.
All inputs are finite; a program needn't handle non-finite values. No bound on the sum of `mask_h` or of `mask_panel` or of `mask_slab` on one device may be relied on, other than what follows from the above.
Results may differ from a plain program's by a relative error of at most 0.018.
Values may be sent and summed in bfloat16 or wider, within the bound.
No kernel may reach another device: no remote copies, remote signals or barrier semaphores. Data moves between devices by JAX's collectives and lax.ppermute only.
A program may use at most 64 MiB of HBM per device.

v0:
```python
import jax
import jax.numpy as jnp
from jax import lax
from jax.sharding import PartitionSpec as P

BS = 64
SECTIONS = 2


def from_root(shard, axis, root):
    mine = lax.axis_index(axis) == root
    return lax.psum(jnp.where(mine, shard, jnp.zeros_like(shard)), axis)


def expand_mask(values, mask):
    row_blocks, col_blocks = mask.shape
    grown = (
        values.reshape(row_blocks, BS, col_blocks, BS) * mask.astype(values.dtype)[:, None, :, None]
    )
    return grown.reshape(row_blocks * BS, col_blocks * BS)


def per_device(hamiltonian, z_panel, z_slab, mask_h, mask_panel, mask_slab, section_blocks):
    inner_h = mask_h.shape[1]
    inner_z = mask_panel.shape[0]
    slab_rows = hamiltonian.shape[0]
    width = z_panel.shape[1]
    h_blocks = expand_mask(hamiltonian, mask_h).reshape(mask_h.shape[0], BS, inner_h, BS)
    panel_blocks = expand_mask(z_panel, mask_panel).reshape(inner_z, BS, width)
    slab_masked = expand_mask(z_slab, mask_slab)
    summed = None
    for section in range(SECTIONS):
        chosen = section_blocks[section]
        owner_col = chosen[0] // inner_h
        picked_h = jnp.take(h_blocks, chosen - owner_col * inner_h, axis=2).reshape(slab_rows, -1)
        panel_h = from_root(picked_h, "col", owner_col)
        owner_row = chosen[0] // inner_z
        picked_z = jnp.take(panel_blocks, chosen - owner_row * inner_z, axis=0).reshape(-1, width)
        panel_z = from_root(picked_z, "row", owner_row)
        contrib = jnp.dot(panel_h, panel_z, preferred_element_type=jnp.float32)
        summed = contrib if summed is None else summed + contrib
    y_tile = summed.astype(jnp.bfloat16)
    y_full = lax.all_gather(y_tile, "col", axis=1, tiled=True)
    return lax.psum_scatter(
        lax.dot_general(
            y_full, slab_masked, (((0,), (0,)), ((), ())), preferred_element_type=jnp.float32
        ).astype(jnp.bfloat16),
        "row",
        scatter_dimension=0,
        tiled=True,
    )


def solution(mesh):
    placed = (
        P("row", "col"),
        P("row", "col"),
        P("row", "col"),
        P("row", "col"),
        P("row", "col"),
        P("row", "col"),
        P(),
    )
    return jax.shard_map(
        per_device, mesh=mesh, in_specs=placed, out_specs=P("row", "col"), check_vma=False
    )
```

profile of v0, /device:TPU:4, one launch (start us, length us, event | category | flops | bytes accessed | tf_op | source)
XLA Modules:
  0.0 709.6 jit_solution(12671105843311034150)
XLA Ops:
  6.5 0.0 copy-start.2
  6.5 0.0 copy-start.3
  6.5 0.0 all-reduce.5.cloned.1.call-start
  6.5 1.3 fusion.2
  12.7 2.1 reshape.52
  14.7 0.0 copy-done.3
  14.8 0.0 copy-done.2
  14.9 0.4 copy_multiply_fusion
  15.2 0.6 gather_fusion.2
  15.9 0.6 gather_fusion
  16.5 0.2 bitcast_select_fusion
  16.7 0.3 copy.11
  17.1 1.1 select_n.70
  18.2 0.0 copy-start.4
  18.2 0.0 copy-start
  18.2 0.3 copy.13
  18.5 1.1 select_n.78
  19.6 0.0 all-reduce.5.cloned.1.call-update
  19.6 0.0 all-reduce.7.cloned.1.call-start
  19.6 0.0 copy-done.4
  19.7 0.1 copy.12
  19.8 0.1 mul.47
  19.9 0.1 mul.48
  20.0 0.0 copy-done
  20.0 0.1 broadcast_multiply_fusion
  20.1 0.6 gather_fusion.3
  20.8 0.6 gather_fusion.1
  21.4 0.9 select_select_fusion
  22.3 0.0 copy-start.5
  22.3 0.0 copy-start.1
  22.3 0.0 all-reduce.7.cloned.1.call-update
  22.3 0.0 all-gather.2.cloned.1.call-start
  22.4 327.7 %all-reduce.5.cloned.1.call-done = (bf16[128,1024]{1,0:T(8,128)(2,1)}, bf16[128,1024]{1,0:T(8,128)(2,1)}) async-done(((bf16[128,1024]{1,0:T(8,128)(2,1)}, bf16[128,1024]{1,0:T(8,128)(2,1)}), (bf16[128,1024]{1,0:T(8,128)(2,1)}, bf16[128,1024]{1,0:T(8,128)(2,1)})) %all-reduce.5.cloned.1.call-update) | async-done | bytes 524304 | tf_op jit(solution)/shard_map/psum | solution.py:12
  350.1 189.1 %all-reduce.7.cloned.1.call-done = (bf16[1024,128]{1,0:T(8,128)(2,1)}, bf16[1024,128]{1,0:T(8,128)(2,1)}) async-done(((bf16[1024,128]{1,0:T(8,128)(2,1)}, bf16[1024,128]{1,0:T(8,128)(2,1)}), (bf16[1024,128]{1,0:T(8,128)(2,1)}, bf16[1024,128]{1,0:T(8,128)(2,1)})) %all-reduce.7.cloned.1.call-update) | async-done | bytes 524304 | tf_op jit(solution)/shard_map/psum | solution.py:12
  539.2 1.2 fusion.3
  540.5 1.9 fusion
  542.3 0.0 all-gather.2.cloned.1.call-update
  542.4 0.0 reduce-scatter.2.cloned.1.call-start
  542.4 0.0 copy-done.5
  542.4 0.1 mul.54
  542.5 0.1 mul.55
  542.6 69.6 %all-gather.2.cloned.1.call-done = bf16[128,4096]{1,0:T(8,128)(2,1)} async-done(((bf16[128,128]{1,0:T(8,128)(2,1)}), bf16[128,4096]{1,0:T(8,128)(2,1)}) %all-gather.2.cloned.1.call-update) | async-done | bytes 1048592 | tf_op jit(solution)/shard_map/all_gather | solution.py:43
  612.2 0.0 copy-done.1
  612.2 2.7 convolution_convert_fusion
  614.9 0.0 reduce-scatter.2.cloned.1.call-update
  614.9 88.1 %reduce-scatter.2.cloned.1.call-done = bf16[256,128]{1,0:T(8,128)(2,1)} async-done(((bf16[4096,128]{1,0:T(8,128)(2,1)}), bf16[256,128]{1,0:T(8,128)(2,1)}) %reduce-scatter.2.cloned.1.call-update) | async-done | bytes 65552 | tf_op jit(solution)/shard_map/reduce_scatter | solution.py:44
  (8 shorter events, 0.1 us)
Async XLA Ops:
  6.5 8.3 %copy-start.2 = (s32[2,16]{1,0:T(2,128)S(1)}, s32[2,16]{1,0:T(2,128)}, u32[]{:S(2)}) copy-start(s32[2,16]{1,0:T(2,128)} %param.17) | copy-start | bytes 388
  6.5 8.2 %copy-start.3 = (s32[2,32]{1,0:T(2,128)S(1)}, s32[2,32]{1,0:T(2,128)}, u32[]{:S(2)}) copy-start(s32[2,32]{1,0:T(2,128)} %param.14) | copy-start | bytes 772
  6.5 343.5 %all-reduce.5.cloned.1.call-start = ((), (), s32[]{:S(2)}) async-start(), calls=%async_computation.3 | async-start | bytes 1048576 | tf_op jit(solution)/shard_map/psum | solution.py:12
  18.2 1.5 copy-start.4
  18.2 1.9 copy-start
  19.6 519.6 %all-reduce.7.cloned.1.call-start = ((), (), s32[]{:S(2)}) async-start(), calls=%async_computation.4 | async-start | bytes 1048576 | tf_op jit(solution)/shard_map/psum | solution.py:12
  22.3 520.1 %copy-start.5 = (s32[2,2]{1,0:T(2,128)S(1)}, s32[2,2]{1,0:T(2,128)}, u32[]{:S(2)}) copy-start(s32[2,2]{1,0:T(2,128)} %param.16) | copy-start | bytes 52
  22.3 589.9 %copy-start.1 = (bf16[128,128]{1,0:T(8,128)(2,1)S(1)}, bf16[128,128]{1,0:T(8,128)(2,1)}, u32[]{:S(2)}) copy-start(bf16[128,128]{1,0:T(8,128)(2,1)} %param.13) | copy-start | bytes 98308
  22.3 589.9 %all-gather.2.cloned.1.call-start = ((), (), s32[]{:S(2)}) async-start(), calls=%async_computation.1 | async-start | bytes 1081344 | tf_op jit(solution)/shard_map/all_gather | solution.py:43
  542.4 160.7 %reduce-scatter.2.cloned.1.call-start = ((), (), s32[]{:S(2)}) async-start(), calls=%async_computation.2 | async-start | bytes 1114112 | tf_op jit(solution)/shard_map/reduce_scatter | solution.py:44
Sparse Core Ops, SparseCore 0:
  19.7 330.2 all-reduce.4
  353.3 185.8 all-reduce.6
  542.5 69.6 all-gather.1
  615.1 87.9 reduce-scatter.1
where the time goes:
time: 710 us
  waiting for transfers between devices  675 us (95%)
  between operations  18.2 us (3%)
  local copies, waits for them, and re-layouts  9.24 us (1%)
    psum x2, waiting for transfers between devices, from_root(): return lax.psum(jnp.where(mine, shard, jnp.zeros_like(shard)), axis)  517 us
    reduce_scatter x1, waiting for transfers between devices, per_device(): lax.psum_scatter(lax.dot_general(y_full, slab_masked, (((0,), (0,)), ((),...  88.1 us
    all_gather x1, waiting for transfers between devices, per_device(): y_full = lax.all_gather(y_tile, 'col', axis=1, tiled=True)  69.6 us
  transfers between devices with their start and end apart: 4, of which 4 were waited for; matrix products, arithmetic and copies ran while one was open for 0% of the time, Pallas kernels for 0%

commit v1 on v0

v1 whole, which is shorter than its diff:
```python
import jax
import jax.numpy as jnp
from jax import lax
from jax.experimental import pallas as pl
from jax.experimental.pallas import tpu as pltpu
from jax.sharding import Mesh, PartitionSpec as P

BS = 64
LANES = 128
SECTIONS = 2
PICKS = 16
H_BLOCKS = 32
Z_BLOCKS = 64
ROW = ("zl", "y")
COL = ("x", "zh", "co")
PLANE = ("y", "x")
ALL = ROW + COL
SIZES = (4, 4, 4, 4, 2)

SMEM = pl.BlockSpec(memory_space=pltpu.SMEM)
VMEM = pl.BlockSpec(memory_space=pltpu.VMEM)


def owner_col(blocks, section):
    return blocks[section, 0] // H_BLOCKS


def owner_row(blocks, section):
    return blocks[section, 0] // Z_BLOCKS


def lane_mask(left, right):
    lane = lax.broadcasted_iota(jnp.int32, (1, LANES), 1)
    return jnp.where(lane < BS, left, right).astype(jnp.float32).astype(jnp.bfloat16)


def rows(index, size):
    return pl.ds(pl.multiple_of(index * size, size), size)


def pick_h_kernel(blocks, mask_h, h, picked, turned):
    me = (lax.axis_index("x") * 4 + lax.axis_index("zh")) * 2 + lax.axis_index("co")
    own = jnp.where(owner_col(blocks, 1) == me, 1, 0)
    for tile in range(h.shape[1] // LANES):
        at = slice(tile * LANES, (tile + 1) * LANES)
        turned[at, :] = h[:, at].T
    for p in range(PICKS):
        b = lax.rem(blocks[own, p], H_BLOCKS)
        picked[p] = turned[rows(b, BS), :] * lane_mask(mask_h[0, b], mask_h[1, b])


def pick_z_kernel(blocks, mask_panel, pair_h, z, packed):
    co = lax.axis_index("co")
    core = lax.rem(owner_col(blocks, co), 2)
    for p in range(PICKS):
        packed[p, 0] = pair_h[core, p]
        for s in range(SECTIONS):
            b = lax.rem(blocks[s, p], Z_BLOCKS)
            packed[p, 1 + s] = z[rows(b, BS), :] * lane_mask(mask_panel[b, 0], mask_panel[b, 1])


def choose_kernel(blocks, got, part_h, part_z):
    x0 = owner_col(blocks, lax.axis_index("co")) // 8
    for y in range(4):
        part_h[y] = got[4 * y + x0, 0]
    for s in range(SECTIONS):
        y0 = lax.rem(owner_row(blocks, s), 4)
        for x in range(4):
            part_z[s, x] = got[4 * y0 + x, 1 + s]


def product_kernel(blocks, all_h, all_z, out):
    z0 = [owner_row(blocks, s) // 4 for s in range(SECTIONS)]
    right = [
        jnp.concatenate([all_z[z0[s], s, x] for s in range(SECTIONS)], axis=0) for x in range(4)
    ]
    for y in range(4):
        left = jnp.concatenate([all_h[s, y] for s in range(SECTIONS)], axis=0)
        for x in range(4):
            out[4 * y + x] = lax.dot_general(
                left, right[x], (((0,), (0,)), ((), ())), preferred_element_type=jnp.float32
            ).astype(out.dtype)


def total_kernel(parts, copies):
    total = parts[0].astype(jnp.float32)
    for i in range(1, parts.shape[0]):
        total = total + parts[i].astype(jnp.float32)
    total = total.astype(copies.dtype)
    for i in range(copies.shape[0]):
        copies[i] = total


def last_kernel(y_col, slabs, out):
    for half in range(2):
        total = jnp.zeros((LANES, LANES), jnp.float32)
        for r in range(16):
            total = total + lax.dot_general(
                y_col[r],
                slabs[2 * r + half],
                (((0,), (0,)), ((), ())),
                preferred_element_type=jnp.float32,
            )
        out[half] = total.astype(out.dtype)


def shape(*dims):
    return jax.ShapeDtypeStruct(dims, jnp.bfloat16)


def expand_mask(values, mask):
    row_blocks, col_blocks = mask.shape
    grown = (
        values.reshape(row_blocks, BS, col_blocks, BS) * mask.astype(values.dtype)[:, None, :, None]
    )
    return grown.reshape(row_blocks * BS, col_blocks * BS)


def swapped_pairs():
    return [
        ((r * 16 + k) * 2 + co, (k * 16 + r) * 2 + co)
        for r in range(16)
        for k in range(16)
        for co in range(2)
    ]


def per_device(hamiltonian, z_panel, z_slab, mask_h, mask_panel, mask_slab, blocks):
    slab = expand_mask(z_slab, mask_slab)
    slab = lax.ppermute(slab, ALL, swapped_pairs())

    own_h = pl.pallas_call(
        pick_h_kernel,
        out_shape=shape(PICKS, BS, LANES),
        in_specs=[SMEM, SMEM, VMEM],
        out_specs=VMEM,
        scratch_shapes=[pltpu.VMEM((hamiltonian.shape[1], LANES), jnp.bfloat16)],
        name="pick_h",
    )(blocks, mask_h, hamiltonian)
    pair_h = lax.all_gather(own_h, "co", axis=0)
    slab, pair_h = lax.optimization_barrier((slab, pair_h))
    slabs = lax.all_gather(slab, COL, axis=0)
    packed = pl.pallas_call(
        pick_z_kernel,
        out_shape=shape(PICKS, 1 + SECTIONS, BS, LANES),
        in_specs=[SMEM, SMEM, VMEM, VMEM],
        out_specs=VMEM,
        name="pick_z",
    )(blocks, mask_panel, pair_h, z_panel)
    got = lax.all_to_all(packed, PLANE, 0, 0, tiled=True)
    part_h, part_z = pl.pallas_call(
        choose_kernel,
        out_shape=(shape(4, BS, LANES), shape(SECTIONS, 4, BS, LANES)),
        in_specs=[SMEM, VMEM],
        out_specs=(VMEM, VMEM),
        name="choose",
    )(blocks, got)
    all_z = lax.all_gather(part_z, "zl", axis=0)
    across = lax.all_gather(part_h, "zh", axis=0)
    zh0 = lax.rem(owner_col(blocks, lax.axis_index("co")) // 2, 4)
    all_h = lax.all_gather(
        lax.dynamic_index_in_dim(across, zh0, 0, keepdims=False), "co", axis=0
    )
    partial = pl.pallas_call(
        product_kernel,
        out_shape=shape(16, LANES, LANES),
        in_specs=[SMEM, VMEM, VMEM],
        out_specs=VMEM,
        name="product",
    )(blocks, all_h, all_z)
    partial = lax.all_to_all(partial, PLANE, 0, 0, tiled=True)
    slabs, partial = lax.optimization_barrier((slabs, partial))
    copies = pl.pallas_call(
        total_kernel,
        out_shape=shape(16, LANES, LANES),
        in_specs=[VMEM],
        out_specs=VMEM,
        name="total",
    )(partial)
    y_col = lax.all_to_all(copies, ROW, 0, 0, tiled=True)
    halves = pl.pallas_call(
        last_kernel,
        out_shape=shape(2, LANES, LANES),
        in_specs=[VMEM, VMEM],
        out_specs=VMEM,
        name="last",
    )(y_col, slabs)
    k_block = lax.all_to_all(halves, "co", 0, 0, tiled=True)
    return lax.ppermute(k_block.reshape(-1, LANES), ALL, swapped_pairs())


def solution(mesh):
    fine = Mesh(mesh.devices.reshape(SIZES), ALL)
    placed = (P(ROW, COL),) * 6 + (P(),)
    return jax.shard_map(
        per_device, mesh=fine, in_specs=placed, out_specs=P(ROW, COL), check_vma=False
    )
```

time: 710 us -> 172 us (0.24)
  the two profiles are of different devices: /device:TPU:4 before, /device:TPU:64 now
where the time goes in v1:
time: 172 us; the launch traced here: 171 us
  blocking collectives  84.9 us (49%)
  waiting for transfers between devices  27.4 us (16%)
  starting transfers between devices  23.9 us (14%)
  between operations  16.1 us (9%)
  Pallas kernels  13.1 us (8%)
  local copies, waits for them, and re-layouts  5 us (3%)
    all_gather x1, blocking collectives, per_device(): all_z = lax.all_gather(part_z, 'zl', axis=0)  20.5 us
    all_gather x1, blocking collectives, per_device(): across = lax.all_gather(part_h, 'zh', axis=0)  19.6 us
    all_to_all x1, blocking collectives, per_device(): y_col = lax.all_to_all(copies, ROW, 0, 0, tiled=True)  18.2 us
    all_to_all x1, starting transfers between devices, per_device(): got = lax.all_to_all(packed, PLANE, 0, 0, tiled=True)  16.7 us
    ppermute x1, waiting for transfers between devices, per_device(): return lax.ppermute(k_block.reshape(-1, LANES), ALL, swapped_pairs())  16.1 us
    all_to_all x1, blocking collectives, per_device(): partial = lax.all_to_all(partial, PLANE, 0, 0, tiled=True)  14.6 us
    all_to_all x1, waiting for transfers between devices, per_device(): got = lax.all_to_all(packed, PLANE, 0, 0, tiled=True)  11.2 us
    all_gather x1, blocking collectives, per_device(): pair_h = lax.all_gather(own_h, 'co', axis=0)  5.08 us
  transfers between devices with their start and end apart: 4, of which 2 were waited for; matrix products, arithmetic and copies ran while one was open for 1% of the time, Pallas kernels for 5%

profile of v1, /device:TPU:64, one launch (start us, length us, event | category | flops | bytes accessed | tf_op | source)
XLA Modules:
  0.0 171.0 jit_solution(17922942370829343793)
XLA Ops:
  6.5 0.0 all-gather.6.cloned.1.call-start
  6.5 0.7 convert_element_type.3
  7.2 0.1 mul.11
  7.3 0.0 copy-start.2
  7.3 0.1 mul.12
  7.4 0.6 copy-done.2
  8.1 4.0 %collective-permute-start = (bf16[128,128]{1,0:T(8,128)(2,1)S(1)}, bf16[128,128]{1,0:T(8,128)(2,1)S(1)}, u32[]{:S(2)}, u32[]{:S(2)}) collective-permute-start(bf16[128,128]{1,0:T(8,128)(2,1)S(1)} %mul.13), channel_id=1, source_target_pairs={{0,0},{1,1},{2,32},{3,33},{4,64},{5,65},{6,96},{7,97},{8,128},{9,1... | collective-permute-start | bytes 98312 | tf_op jit(solution)/shard_map/ppermute | solution.py:130
  12.1 2.0 %pick_h.1 = bf16[16,64,128]{2,1,0:T(8,128)(2,1)} custom-call(s32[2,16]{1,0:T(2,128)} %blocks.7, s32[2,32]{1,0:T(2,128)} %mask_h.1, bf16[128,2048]{1,0:T(8,128)(2,1)} %h.1), custom_call_target="tpu_custom_call" | custom-call | tf_op jit(solution)/shard_map/pick_h/pallas_call | solution.py:132
  14.1 5.1 %all-gather = bf16[32,64,128]{2,1,0:T(8,128)(2,1)} all-gather(bf16[16,64,128]{2,1,0:T(8,128)(2,1)} %pick_h.1), channel_id=2, replica_groups=mesh['zl'=4,'y'=4,'x'=4,'zh'=4,'co'=2] {'co'}, dimensions={0}, use_global_device_ids=true | all-gather | bytes 786432 | tf_op jit(solution)/shard_map/all_gather | solution.py:140
  19.2 0.0 collective-permute-done
  19.2 0.0 copy-start.3
  19.2 0.0 copy-start.5
  19.2 0.6 copy-done.3
  19.8 0.0 all-gather.6.cloned.1.call-update
  19.8 0.1 copy-done.5
  19.9 0.7 copy.9.mask_panel
  20.6 2.5 %pick_z.1 = bf16[16,3,64,128]{3,2,1,0:T(8,128)(2,1)} custom-call(s32[2,16]{1,0:T(2,128)} %blocks.7, s32[64,2]{1,0:T(8,128)} %copy.9.mask_panel, bf16[2,16,64,128]{3,2,1,0:T(8,128)(2,1)} %bitcast.7, bf16[4096,128]{1,0:T(8,128)(2,1)} %z.1), custom_call_target="tpu_custom_call" | custom-call | tf_op jit(solution)/shard_map/pick_z/pallas_call | solution.py:143
  23.1 16.7 %all-to-all-start = ((bf16[16,3,64,128]{3,2,1,0:T(8,128)(2,1)}), bf16[16,3,64,128]{3,2,1,0:T(8,128)(2,1)S(1)}, u32[]{:S(2)}, u32[]{:S(2)}) async-start(bf16[16,3,64,128]{3,2,1,0:T(8,128)(2,1)} %pick_z.1), calls=%async_computation | async-start | bytes 1572864 | tf_op jit(solution)/shard_map/all_to_all | solution.py:150
  39.8 0.0 copy-start.4
  39.8 0.7 copy-done.4
  40.5 0.5 constant_dynamic-slice_fusion.1
  43.7 11.2 %all-to-all-done.got = bf16[16,3,64,128]{3,2,1,0:T(8,128)(2,1)S(1)} async-done(((bf16[16,3,64,128]{3,2,1,0:T(8,128)(2,1)}), bf16[16,3,64,128]{3,2,1,0:T(8,128)(2,1)S(1)}, u32[]{:S(2)}, u32[]{:S(2)}) %all-to-all-start) | async-done | bytes 786464 | tf_op jit(solution)/shard_map/all_to_all | solution.py:150
  54.9 0.0 copy-start
  54.9 0.9 copy-done
  55.9 1.8 %choose.1 = (bf16[4,64,128]{2,1,0:T(8,128)(2,1)}, bf16[2,4,64,128]{3,2,1,0:T(8,128)(2,1)}) custom-call(s32[2,16]{1,0:T(2,128)} %blocks.7, bf16[16,3,64,128]{3,2,1,0:T(8,128)(2,1)} %copy-done), custom_call_target="tpu_custom_call" | custom-call | tf_op jit(solution)/shard_map/choose/pallas_call | solution.py:151
  57.7 19.6 %all-gather.2 = bf16[16,64,128]{2,1,0:T(8,128)(2,1)S(1)} all-gather(bf16[4,64,128]{2,1,0:T(8,128)(2,1)} %get-tuple-element.13), channel_id=4, replica_groups=mesh['zl'=4,'y'=4,'x'=4,'zh'=4,'co'=2] {'zh'}, dimensions={0}, use_global_device_ids=true | all-gather | bytes 327680 | tf_op jit(solution)/shard_map/all_gather | solution.py:159
  77.3 0.0 copy-start.1
  77.3 2.2 %all_gather.34.all_h = bf16[2,4,64,128]{3,2,1,0:T(8,128)(2,1)} all-gather(bf16[1,4,64,128]{3,2,1,0:T(8,128)(2,1)S(1)} %constant_dynamic-slice_fusion), channel_id=1, replica_groups=mesh['zl'=4,'y'=4,'x'=4,'zh'=4,'co'=2] {'co'}, dimensions={0}, use_global_device_ids=true | all-gather | bytes 196608 | tf_op jit(solution)/shard_map/all_gather | solution.py:161
  79.5 0.0 copy-done.1
  79.5 20.5 %all-gather.3 = bf16[8,4,64,128]{3,2,1,0:T(8,128)(2,1)} all-gather(bf16[2,4,64,128]{3,2,1,0:T(8,128)(2,1)S(1)} %copy-done.1), channel_id=5, replica_groups=mesh['zl'=4,'y'=4,'x'=4,'zh'=4,'co'=2] {'zl'}, dimensions={0}, use_global_device_ids=true | all-gather | bytes 655360 | tf_op jit(solution)/shard_map/all_gather | solution.py:158
  100.0 2.3 %product.1 = bf16[16,128,128]{2,1,0:T(8,128)(2,1)} custom-call(s32[2,16]{1,0:T(2,128)} %blocks.7, bf16[2,4,64,128]{3,2,1,0:T(8,128)(2,1)} %all_gather.34.all_h, bf16[4,2,4,64,128]{4,3,2,1,0:T(8,128)(2,1)} %bitcast.6), custom_call_target="tpu_custom_call" | custom-call | tf_op jit(solution)/shard_map/product/pallas_call | solution.py:164
  102.3 14.6 %all_to_all.20.parts = bf16[16,128,128]{2,1,0:T(8,128)(2,1)} all-to-all(bf16[16,128,128]{2,1,0:T(8,128)(2,1)} %product.1), channel_id=1, replica_groups=mesh['zl'=4,'y'=4,'x'=4,'zh'=4,'co'=2] {'y','x'}, dimensions={0} | all-to-all | bytes 1048576 | tf_op jit(solution)/shard_map/all_to_all | solution.py:171
  116.9 0.0 all-gather.6.cloned.1.call-done
  116.9 2.0 %total.1 = bf16[16,128,128]{2,1,0:T(8,128)(2,1)} custom-call(bf16[16,128,128]{2,1,0:T(8,128)(2,1)} %all_to_all.20.parts), custom_call_target="tpu_custom_call" | custom-call | tf_op jit(solution)/shard_map/total/pallas_call | solution.py:173
  118.9 18.2 %all_to_all.21.y_col = bf16[16,128,128]{2,1,0:T(8,128)(2,1)} all-to-all(bf16[16,128,128]{2,1,0:T(8,128)(2,1)} %total.1), channel_id=1, replica_groups=mesh['zl'=4,'y'=4,'x'=4,'zh'=4,'co'=2] {'zl','y'}, dimensions={0} | all-to-all | bytes 1048576 | tf_op jit(solution)/shard_map/all_to_all | solution.py:180
  137.1 2.5 %last.1 = bf16[2,128,128]{2,1,0:T(8,128)(2,1)} custom-call(bf16[16,128,128]{2,1,0:T(8,128)(2,1)} %all_to_all.21.y_col, bf16[32,128,128]{2,1,0:T(8,128)(2,1)} %bitcast.8), custom_call_target="tpu_custom_call" | custom-call | tf_op jit(solution)/shard_map/last/pallas_call | solution.py:181
  139.6 4.7 %all_to_all.22 = bf16[2,128,128]{2,1,0:T(8,128)(2,1)S(1)} all-to-all(bf16[2,128,128]{2,1,0:T(8,128)(2,1)} %last.1), channel_id=1, replica_groups=mesh['zl'=4,'y'=4,'x'=4,'zh'=4,'co'=2] {'co'}, dimensions={0} | all-to-all | bytes 131072 | tf_op jit(solution)/shard_map/all_to_all | solution.py:188
  144.3 3.1 %collective-permute-start.1 = (bf16[256,128]{1,0:T(8,128)(2,1)S(1)}, bf16[256,128]{1,0:T(8,128)(2,1)S(1)}, u32[]{:S(2)}, u32[]{:S(2)}) collective-permute-start(bf16[256,128]{1,0:T(8,128)(2,1)S(1)} %bitcast.10), channel_id=1, source_target_pairs={{0,0},{1,1},{2,32},{3,33},{4,64},{5,65},{6,96},{7,97},{8,128},{9,1... | collective-permute-start | bytes 196616 | tf_op jit(solution)/shard_map/ppermute | solution.py:189
  147.4 16.1 %collective-permute-done.1 = bf16[256,128]{1,0:T(8,128)(2,1)S(1)} collective-permute-done((bf16[256,128]{1,0:T(8,128)(2,1)S(1)}, bf16[256,128]{1,0:T(8,128)(2,1)S(1)}, u32[]{:S(2)}, u32[]{:S(2)}) %collective-permute-start.1) | collective-permute-done | bytes 65568 | tf_op jit(solution)/shard_map/ppermute | solution.py:189
  163.5 0.6 copy.11
  (2 shorter events, 0.0 us)
Async XLA Ops:
  6.5 110.4 %all-gather.6.cloned.1.call-start = ((), (), s32[]{:S(2)}) async-start(), calls=%async_computation.4 | async-start | bytes 1081344 | tf_op jit(solution)/shard_map/all_gather | solution.py:142
  7.3 0.8 copy-start.2
  8.1 11.1 %collective-permute-start = (bf16[128,128]{1,0:T(8,128)(2,1)S(1)}, bf16[128,128]{1,0:T(8,128)(2,1)S(1)}, u32[]{:S(2)}, u32[]{:S(2)}) collective-permute-start(bf16[128,128]{1,0:T(8,128)(2,1)S(1)} %mul.13), channel_id=1, source_target_pairs={{0,0},{1,1},{2,32},{3,33},{4,64},{5,65},{6,96},{7,97},{8,128},{9,1... | collective-permute-start | bytes 98312 | tf_op jit(solution)/shard_map/ppermute | solution.py:130
  19.2 0.6 copy-start.3
  19.2 0.7 copy-start.5
  23.1 31.8 %all-to-all-start = ((bf16[16,3,64,128]{3,2,1,0:T(8,128)(2,1)}), bf16[16,3,64,128]{3,2,1,0:T(8,128)(2,1)S(1)}, u32[]{:S(2)}, u32[]{:S(2)}) async-start(bf16[16,3,64,128]{3,2,1,0:T(8,128)(2,1)} %pick_z.1), calls=%async_computation | async-start | bytes 1572864 | tf_op jit(solution)/shard_map/all_to_all | solution.py:150
  39.8 0.7 copy-start.4
  54.9 0.9 copy-start
  77.3 2.2 %copy-start.1 = (bf16[2,4,64,128]{3,2,1,0:T(8,128)(2,1)S(1)}, bf16[2,4,64,128]{3,2,1,0:T(8,128)(2,1)}, u32[]{:S(2)}) copy-start(bf16[2,4,64,128]{3,2,1,0:T(8,128)(2,1)} %get-tuple-element.14) | copy-start | bytes 393220
  144.3 19.2 %collective-permute-start.1 = (bf16[256,128]{1,0:T(8,128)(2,1)S(1)}, bf16[256,128]{1,0:T(8,128)(2,1)S(1)}, u32[]{:S(2)}, u32[]{:S(2)}) collective-permute-start(bf16[256,128]{1,0:T(8,128)(2,1)S(1)} %bitcast.10), channel_id=1, source_target_pairs={{0,0},{1,1},{2,32},{3,33},{4,64},{5,65},{6,96},{7,97},{8,128},{9,1... | collective-permute-start | bytes 196616 | tf_op jit(solution)/shard_map/ppermute | solution.py:189
Sparse Core Ops, SparseCore 0:
  20.0 79.4 all-gather.5

commit v2 on v1

v2 whole, which is shorter than its diff:
```python
import jax
import jax.numpy as jnp
from jax import lax
from jax.experimental import pallas as pl
from jax.experimental.pallas import tpu as pltpu
from jax.sharding import Mesh, PartitionSpec as P

BS = 64
LANES = 128
SECTIONS = 2
PICKS = 16
H_BLOCKS = 32
Z_BLOCKS = 64
ROW = ("zl", "y")
COL = ("x", "zh", "co")
PLANE = ("y", "x")
ALL = ROW + COL
SIZES = (4, 4, 4, 4, 2)

SMEM = pl.BlockSpec(memory_space=pltpu.SMEM)
VMEM = pl.BlockSpec(memory_space=pltpu.VMEM)


def owner_col(blocks, section):
    return blocks[section, 0] // H_BLOCKS


def owner_row(blocks, section):
    return blocks[section, 0] // Z_BLOCKS


def lane_mask(left, right):
    lane = lax.broadcasted_iota(jnp.int32, (1, LANES), 1)
    return jnp.where(lane < BS, left, right).astype(jnp.float32).astype(jnp.bfloat16)


def rows(index, size):
    return pl.ds(pl.multiple_of(index * size, size), size)


def pick_kernel(blocks, mask_h, mask_panel, mask_slab, h, z, slab, packed, masked, turned):
    me = (lax.axis_index("x") * 4 + lax.axis_index("zh")) * 2 + lax.axis_index("co")
    own = jnp.where(owner_col(blocks, 1) == me, 1, 0)
    for tile in range(h.shape[1] // LANES):
        at = slice(tile * LANES, (tile + 1) * LANES)
        turned[at, :] = h[:, at].T
    for p in range(PICKS):
        b = lax.rem(blocks[own, p], H_BLOCKS)
        packed[p, 0] = turned[rows(b, BS), :] * lane_mask(mask_h[0, b], mask_h[1, b])
        for s in range(SECTIONS):
            b = lax.rem(blocks[s, p], Z_BLOCKS)
            packed[p, 1 + s] = z[rows(b, BS), :] * lane_mask(mask_panel[0, b], mask_panel[1, b])
    for i in range(2):
        at = slice(i * BS, (i + 1) * BS)
        masked[i] = slab[at, :] * lane_mask(mask_slab[i, 0], mask_slab[i, 1])


def choose_kernel(blocks, got, part_h, part_z):
    for s in range(SECTIONS):
        x0 = owner_col(blocks, s) // 8
        y0 = lax.rem(owner_row(blocks, s), 4)
        for i in range(4):
            part_h[s, i] = got[4 * i + x0, 0]
            block = got[4 * y0 + i, 1 + s]
            for copy in range(4):
                part_z[copy, s, i] = block


def product_kernel(blocks, pair, all_z, out):
    z0 = [owner_row(blocks, s) // 4 for s in range(SECTIONS)]
    right = [
        jnp.concatenate([all_z[z0[s], s, x] for s in range(SECTIONS)], axis=0) for x in range(4)
    ]
    for y in range(4):
        left = jnp.concatenate([pair[s, y] for s in range(SECTIONS)], axis=0)
        for x in range(4):
            out[4 * y + x] = lax.dot_general(
                left, right[x], (((0,), (0,)), ((), ())), preferred_element_type=jnp.float32
            ).astype(out.dtype)


def total_kernel(parts, copies):
    total = parts[0].astype(jnp.float32)
    for i in range(1, parts.shape[0]):
        total = total + parts[i].astype(jnp.float32)
    total = total.astype(copies.dtype)
    for i in range(copies.shape[0]):
        copies[i] = total


def last_kernel(y_col, *slabs_and_out):
    slabs, out = slabs_and_out[:-1], slabs_and_out[-1]
    for core in range(2):
        total = jnp.zeros((LANES, LANES), jnp.float32)
        for back, slab in zip((0, 1, 3, 2), slabs):
            x = lax.rem(lax.axis_index("x") + 4 - back, 4)
            for zh in range(4):
                right = jnp.concatenate([slab[core, 2 * zh + i] for i in range(2)], axis=0)
                total = total + lax.dot_general(
                    y_col[4 * x + zh],
                    right,
                    (((0,), (0,)), ((), ())),
                    preferred_element_type=jnp.float32,
                )
        out[core] = total.astype(out.dtype)


def shape(*dims):
    return jax.ShapeDtypeStruct(dims, jnp.bfloat16)


def swapped_pairs():
    return [
        ((r * 16 + k) * 2 + co, (k * 16 + r) * 2 + co)
        for r in range(16)
        for k in range(16)
        for co in range(2)
    ]


def per_device(hamiltonian, z_panel, z_slab, mask_h, mask_panel, mask_slab, blocks):
    packed, slab = pl.pallas_call(
        pick_kernel,
        out_shape=(shape(PICKS, 1 + SECTIONS, BS, LANES), shape(2, BS, LANES)),
        in_specs=[SMEM] * 4 + [VMEM] * 3,
        out_specs=(VMEM, VMEM),
        scratch_shapes=[pltpu.VMEM((hamiltonian.shape[1], LANES), jnp.bfloat16)],
        name="pick",
    )(blocks, mask_h, mask_panel.T, mask_slab, hamiltonian, z_panel, z_slab)
    slab = lax.ppermute(slab, ALL, swapped_pairs())
    got = lax.all_to_all(packed, PLANE, 0, 0, tiled=True)
    slab, got = lax.optimization_barrier((slab, got))
    part_h, part_z = pl.pallas_call(
        choose_kernel,
        out_shape=(shape(SECTIONS, 4, BS, LANES), shape(4, SECTIONS, 4, BS, LANES)),
        in_specs=[SMEM, VMEM],
        out_specs=(VMEM, VMEM),
        name="choose",
    )(blocks, got)
    all_z = lax.all_to_all(part_z, "zl", 0, 0, tiled=True)
    core = lax.axis_index("co")
    first = jnp.where(core == 0, blocks[0, 0], blocks[1, 0])
    owner_core = lax.shift_right_logical(first, 5) & 1
    owner_zh = lax.shift_right_logical(first, 6) & 3
    pair_h = lax.all_gather(part_h, "co", axis=0)
    mine_h = lax.dynamic_slice(
        pair_h, (owner_core, core, 0, 0, 0), (1, 1) + part_h.shape[1:]
    )
    across = lax.all_gather(jnp.concatenate([mine_h[0, 0], slab], axis=0), "zh", axis=0)
    from_owner = lax.dynamic_index_in_dim(across[:, :4], owner_zh, 0, keepdims=False)
    pair = lax.all_gather(
        jnp.concatenate([from_owner, across[:, 4:].reshape(8, BS, LANES)], axis=0), "co", axis=0
    )
    partial = pl.pallas_call(
        product_kernel,
        out_shape=shape(16, LANES, LANES),
        in_specs=[SMEM, VMEM, VMEM],
        out_specs=VMEM,
        name="product",
    )(blocks, pair, all_z)
    partial = lax.all_to_all(partial, PLANE, 0, 0, tiled=True)
    slabs = [pair[:, 4:]]
    for back in (1, 3, 2):
        slabs.append(lax.ppermute(slabs[0], "x", [(x, (x + back) % 4) for x in range(4)]))
    slabs[1], slabs[2], partial = lax.optimization_barrier((slabs[1], slabs[2], partial))
    copies = pl.pallas_call(
        total_kernel,
        out_shape=shape(16, LANES, LANES),
        in_specs=[VMEM],
        out_specs=VMEM,
        name="total",
    )(partial)
    y_col = lax.all_to_all(copies, ROW, 0, 0, tiled=True)
    halves = pl.pallas_call(
        last_kernel,
        out_shape=shape(2, LANES, LANES),
        in_specs=[VMEM] * 5,
        out_specs=VMEM,
        name="last",
    )(y_col, *slabs)
    k_block = lax.all_to_all(halves, "co", 0, 0, tiled=True)
    return lax.ppermute(k_block.reshape(-1, LANES), ALL, swapped_pairs())


def solution(mesh):
    fine = Mesh(mesh.devices.reshape(SIZES), ALL)
    placed = (P(ROW, COL),) * 6 + (P(),)
    return jax.shard_map(
        per_device, mesh=fine, in_specs=placed, out_specs=P(ROW, COL), check_vma=False
    )
```

time: 172 us -> 152 us (0.88)
  blocking collectives: 84.9 us -> 40.7 us
  starting transfers between devices: 23.9 us -> 48.8 us
  waiting for transfers between devices: 27.4 us -> 43.2 us
  between operations: 16.1 us -> 1.49 us
    all_to_all x2 -> x0, blocking collectives: 32.8 us -> none  [the longest x1 18.2 us: per_device(): y_col = lax.all_to_all(copies, ROW, 0, 0, tiled=True)]
    all_to_all x0 -> x3, starting transfers between devices: none -> 21.4 us  [the longest x1 9.08 us: per_device(): partial = lax.all_to_all(partial, PLANE, 0, 0, tiled=True)]
    ppermute x0 -> x3, waiting for transfers between devices: none -> 15.3 us  [per_device(): lax.ppermute(slabs[0], 'x', [(x, (x + back) % 4) for x in range(4)])]
    all_gather x4 -> x3, blocking collectives: 47.4 us -> 36 us  [the longest x1 31.8 us: per_device(): lax.all_gather(jnp.concatenate([mine_h[0, 0], slab], axis=0), 'zh', axis=0)]
    ppermute x0 -> x3, starting transfers between devices: none -> 10.4 us  [per_device(): lax.ppermute(slabs[0], 'x', [(x, (x + back) % 4) for x in range(4)])]
    all_to_all x1, starting transfers between devices: 16.7 us -> 7.17 us  [per_device(): got = lax.all_to_all(packed, PLANE, 0, 0, tiled=True)]
    all_to_all x1, waiting for transfers between devices: 11.2 us -> 5.1 us  [per_device(): got = lax.all_to_all(packed, PLANE, 0, 0, tiled=True)]
    all_to_all x0 -> x3, waiting for transfers between devices: none -> 3.64 us  [the longest x1 3.63 us: per_device(): y_col = lax.all_to_all(copies, ROW, 0, 0, tiled=True)]
  transfers between devices with their start and end apart: 4 -> 9, of which waited for: 2 -> 6; matrix products, arithmetic and copies ran while one was open for 1% -> 0% of each run, Pallas kernels for 5% -> 0%
where the time goes in v2:
time: 152 us; the launch traced here: 151 us
  starting transfers between devices  48.8 us (32%)
  waiting for transfers between devices  43.2 us (28%)
  blocking collectives  40.7 us (27%)
  Pallas kernels  11.5 us (8%)
  local copies, waits for them, and re-layouts  5.32 us (4%)
    all_gather x1, blocking collectives, per_device(): lax.all_gather(jnp.concatenate([mine_h[0, 0], slab], axis=0), 'zh', axis=0)  31.8 us
    ppermute x1, waiting for transfers between devices, per_device(): return lax.ppermute(k_block.reshape(-1, LANES), ALL, swapped_pairs())  16.1 us
    ppermute x3, waiting for transfers between devices, per_device(): lax.ppermute(slabs[0], 'x', [(x, (x + back) % 4) for x in range(4)])  15.3 us
    ppermute x3, starting transfers between devices, per_device(): lax.ppermute(slabs[0], 'x', [(x, (x + back) % 4) for x in range(4)])  10.4 us
    all_to_all x1, starting transfers between devices, per_device(): partial = lax.all_to_all(partial, PLANE, 0, 0, tiled=True)  9.08 us
    all_to_all x1, starting transfers between devices, per_device(): got = lax.all_to_all(packed, PLANE, 0, 0, tiled=True)  7.17 us
    all_to_all x1, starting transfers between devices, per_device(): y_col = lax.all_to_all(copies, ROW, 0, 0, tiled=True)  6.62 us
    ppermute x1, starting transfers between devices, per_device(): slab = lax.ppermute(slab, ALL, swapped_pairs())  6.26 us
  transfers between devices with their start and end apart: 9, of which 6 were waited for; matrix products, arithmetic and copies ran while one was open for 0% of the time, Pallas kernels for 0%

profile of v2, /device:TPU:64, one launch (start us, length us, event | category | flops | bytes accessed | tf_op | source)
XLA Modules:
  0.0 151.0 jit_solution(4883959248343624563)
XLA Ops:
  0.0 2.6 %pick.1 = (bf16[16,3,64,128]{3,2,1,0:T(8,128)(2,1)}, bf16[2,64,128]{2,1,0:T(8,128)(2,1)}) custom-call(s32[2,16]{1,0:T(2,128)} %blocks.5, s32[2,32]{1,0:T(2,128)} %mask_h.1, s32[2,64]{1,0:T(2,128)} %bitcast.19, s32[2,2]{1,0:T(2,128)} %mask_slab.1, bf16[128,2048]{1,0:T(8,128)(2,1)} %h.1, bf16[4096,128]{1,0:T(8,128)(2,1)} %z.1, bf16[128,128]{1,0:T(8,128)(2,1)} %slab.1), custom_call_target="tpu_custom_call" | custom-call | tf_op jit(solution)/shard_map/pick/pallas_call | solution.py:122
  2.6 0.0 copy-start.11
  2.6 7.2 %all-to-all-start = ((bf16[16,3,64,128]{3,2,1,0:T(8,128)(2,1)}), bf16[16,3,64,128]{3,2,1,0:T(8,128)(2,1)S(1)}, u32[]{:S(2)}, u32[]{:S(2)}) async-start(bf16[16,3,64,128]{3,2,1,0:T(8,128)(2,1)} %get-tuple-element.15), calls=%async_computation | async-start | bytes 1572864 | tf_op jit(solution)/shard_map/all_to_all | solution.py:131
  9.8 0.0 copy-done.11
  9.8 6.3 %collective-permute-start = (bf16[2,64,128]{2,1,0:T(8,128)(2,1)S(1)}, bf16[2,64,128]{2,1,0:T(8,128)(2,1)S(1)}, u32[]{:S(2)}, u32[]{:S(2)}) collective-permute-start(bf16[2,64,128]{2,1,0:T(8,128)(2,1)S(1)} %copy-done.11), channel_id=1, source_target_pairs={{0,0},{1,1},{2,32},{3,33},{4,64},{5,65},{6,96},{7,97},{8,128},{9,1... | collective-permute-start | bytes 98312 | tf_op jit(solution)/shard_map/ppermute | solution.py:130
  16.1 3.1 %collective-permute-done = bf16[2,64,128]{2,1,0:T(8,128)(2,1)S(1)} collective-permute-done((bf16[2,64,128]{2,1,0:T(8,128)(2,1)S(1)}, bf16[2,64,128]{2,1,0:T(8,128)(2,1)S(1)}, u32[]{:S(2)}, u32[]{:S(2)}) %collective-permute-start) | collective-permute-done | bytes 32800 | tf_op jit(solution)/shard_map/ppermute | solution.py:130
  19.2 5.1 %all-to-all-done.got = bf16[16,3,64,128]{3,2,1,0:T(8,128)(2,1)S(1)} async-done(((bf16[16,3,64,128]{3,2,1,0:T(8,128)(2,1)}), bf16[16,3,64,128]{3,2,1,0:T(8,128)(2,1)S(1)}, u32[]{:S(2)}, u32[]{:S(2)}) %all-to-all-start) | async-done | bytes 786464 | tf_op jit(solution)/shard_map/all_to_all | solution.py:131
  24.3 0.0 copy-start
  24.3 0.9 copy-done
  25.2 2.1 %choose.1 = (bf16[2,4,64,128]{3,2,1,0:T(8,128)(2,1)}, bf16[4,2,4,64,128]{4,3,2,1,0:T(8,128)(2,1)}) custom-call(s32[2,16]{1,0:T(2,128)} %blocks.5, bf16[16,3,64,128]{3,2,1,0:T(8,128)(2,1)} %copy-done), custom_call_target="tpu_custom_call" | custom-call | tf_op jit(solution)/shard_map/choose/pallas_call | solution.py:133
  27.3 0.0 copy-start.9
  27.3 5.7 %all-to-all-start.1 = ((bf16[4,2,4,64,128]{4,3,2,1,0:T(8,128)(2,1)}), bf16[4,2,4,64,128]{4,3,2,1,0:T(8,128)(2,1)S(1)}, u32[]{:S(2)}, u32[]{:S(2)}) async-start(bf16[4,2,4,64,128]{4,3,2,1,0:T(8,128)(2,1)} %get-tuple-element.19), calls=%async_computation.1 | async-start | bytes 1048576 | tf_op jit(solution)/shard_map/all_to_all | solution.py:140
  33.0 0.0 copy-start.10
  33.0 0.7 copy-done.10
  33.7 0.6 fusion
  35.6 0.0 copy-done.9
  35.6 2.0 %all-gather = bf16[4,4,64,128]{3,2,1,0:T(8,128)(2,1)S(1)} all-gather(bf16[2,4,64,128]{3,2,1,0:T(8,128)(2,1)S(1)} %copy-done.9), channel_id=2, replica_groups=mesh['zl'=4,'y'=4,'x'=4,'zh'=4,'co'=2] {'co'}, dimensions={0}, use_global_device_ids=true | all-gather | bytes 393216 | tf_op jit(solution)/shard_map/all_gather | solution.py:145
  37.6 31.8 %all-gather.1 = bf16[24,64,128]{2,1,0:T(8,128)(2,1)S(1)} all-gather(bf16[6,64,128]{2,1,0:T(8,128)(2,1)S(1)} %pad_maximum_fusion.1), channel_id=3, replica_groups=mesh['zl'=4,'y'=4,'x'=4,'zh'=4,'co'=2] {'zh'}, dimensions={0}, use_global_device_ids=true | all-gather | bytes 491520 | tf_op jit(solution)/shard_map/all_gather | solution.py:149
  69.5 2.2 %all-gather.2 = bf16[24,64,128]{2,1,0:T(8,128)(2,1)} all-gather(bf16[12,64,128]{2,1,0:T(8,128)(2,1)S(1)} %pad_maximum_fusion), channel_id=4, replica_groups=mesh['zl'=4,'y'=4,'x'=4,'zh'=4,'co'=2] {'co'}, dimensions={0}, use_global_device_ids=true | all-gather | bytes 589824 | tf_op jit(solution)/shard_map/all_gather | solution.py:151
  71.7 0.0 all-to-all-done.1.all_z
  71.7 0.0 copy-start.3
  71.7 0.8 copy-done.3
  72.5 2.3 %product.1 = bf16[16,128,128]{2,1,0:T(8,128)(2,1)} custom-call(s32[2,16]{1,0:T(2,128)} %blocks.5, bf16[2,12,64,128]{3,2,1,0:T(8,128)(2,1)} %bitcast.12, bf16[4,2,4,64,128]{4,3,2,1,0:T(8,128)(2,1)} %copy-done.3), custom_call_target="tpu_custom_call" | custom-call | tf_op jit(solution)/shard_map/product/pallas_call | solution.py:154
  74.8 9.1 %all-to-all-start.2 = ((bf16[16,128,128]{2,1,0:T(8,128)(2,1)}), bf16[16,128,128]{2,1,0:T(8,128)(2,1)S(1)}, u32[]{:S(2)}, u32[]{:S(2)}) async-start(bf16[16,128,128]{2,1,0:T(8,128)(2,1)} %product.1), calls=%async_computation.2 | async-start | bytes 1048576 | tf_op jit(solution)/shard_map/all_to_all | solution.py:161
  83.9 0.0 copy-done.1
  84.0 0.0 copy-start.5
  84.0 3.8 %collective-permute-start.1 = (bf16[2,8,64,128]{3,2,1,0:T(8,128)(2,1)S(1)}, bf16[2,8,64,128]{3,2,1,0:T(8,128)(2,1)S(1)}, u32[]{:S(2)}, u32[]{:S(2)}) collective-permute-start(bf16[2,8,64,128]{3,2,1,0:T(8,128)(2,1)S(1)} %slice.22.slabs_and_out_0_), channel_id=1, source_target_pairs={{0,8},{8,16},{16,24},{24,0},{1,9},{9,17},{17,25},{25,1},{2,10},{10... | collective-permute-start | bytes 786440 | tf_op jit(solution)/shard_map/ppermute | solution.py:164
  87.8 3.2 %collective-permute-start.2 = (bf16[2,8,64,128]{3,2,1,0:T(8,128)(2,1)S(1)}, bf16[2,8,64,128]{3,2,1,0:T(8,128)(2,1)S(1)}, u32[]{:S(2)}, u32[]{:S(2)}) collective-permute-start(bf16[2,8,64,128]{3,2,1,0:T(8,128)(2,1)S(1)} %slice.22.slabs_and_out_0_), channel_id=1, source_target_pairs={{0,24},{8,0},{16,8},{24,16},{1,25},{9,1},{17,9},{25,17},{2,26},{10... | collective-permute-start | bytes 786440 | tf_op jit(solution)/shard_map/ppermute | solution.py:164
  91.0 7.9 %collective-permute-done.1.slabs_and_out_1_ = bf16[2,8,64,128]{3,2,1,0:T(8,128)(2,1)S(1)} collective-permute-done((bf16[2,8,64,128]{3,2,1,0:T(8,128)(2,1)S(1)}, bf16[2,8,64,128]{3,2,1,0:T(8,128)(2,1)S(1)}, u32[]{:S(2)}, u32[]{:S(2)}) %collective-permute-start.1) | collective-permute-done | bytes 262176 | tf_op jit(solution)/shard_map/ppermute | solution.py:164
  98.9 0.0 collective-permute-done.2.slabs_and_out_2_
  98.9 0.0 all-to-all-done.2.parts
  98.9 0.0 copy-start.4
  98.9 0.8 copy-done.4
  99.8 1.9 %total.1 = bf16[16,128,128]{2,1,0:T(8,128)(2,1)} custom-call(bf16[16,128,128]{2,1,0:T(8,128)(2,1)} %copy-done.4), custom_call_target="tpu_custom_call" | custom-call | tf_op jit(solution)/shard_map/total/pallas_call | solution.py:166
  101.7 0.0 copy-done.6
  101.7 0.0 copy-done.7
  101.7 6.6 %all-to-all-start.3 = ((bf16[16,128,128]{2,1,0:T(8,128)(2,1)}), bf16[16,128,128]{2,1,0:T(8,128)(2,1)S(1)}, u32[]{:S(2)}, u32[]{:S(2)}) async-start(bf16[16,128,128]{2,1,0:T(8,128)(2,1)} %total.1), calls=%async_computation.3 | async-start | bytes 1048576 | tf_op jit(solution)/shard_map/all_to_all | solution.py:173
  108.4 0.0 copy-done.5
  108.4 3.4 %collective-permute-start.3 = (bf16[2,8,64,128]{3,2,1,0:T(8,128)(2,1)S(1)}, bf16[2,8,64,128]{3,2,1,0:T(8,128)(2,1)S(1)}, u32[]{:S(2)}, u32[]{:S(2)}) collective-permute-start(bf16[2,8,64,128]{3,2,1,0:T(8,128)(2,1)S(1)} %slice.22.slabs_and_out_0_), channel_id=1, source_target_pairs={{0,16},{8,24},{16,0},{24,8},{1,17},{9,25},{17,1},{25,9},{2,18},{10... | collective-permute-start | bytes 786440 | tf_op jit(solution)/shard_map/ppermute | solution.py:164
  111.8 7.4 %collective-permute-done.3.slabs_and_out_3_ = bf16[2,8,64,128]{3,2,1,0:T(8,128)(2,1)S(1)} collective-permute-done((bf16[2,8,64,128]{3,2,1,0:T(8,128)(2,1)S(1)}, bf16[2,8,64,128]{3,2,1,0:T(8,128)(2,1)S(1)}, u32[]{:S(2)}, u32[]{:S(2)}) %collective-permute-start.3) | collective-permute-done | bytes 262176 | tf_op jit(solution)/shard_map/ppermute | solution.py:164
  119.1 3.6 %all-to-all-done.3.y_col = bf16[16,128,128]{2,1,0:T(8,128)(2,1)S(1)} async-done(((bf16[16,128,128]{2,1,0:T(8,128)(2,1)}), bf16[16,128,128]{2,1,0:T(8,128)(2,1)S(1)}, u32[]{:S(2)}, u32[]{:S(2)}) %all-to-all-start.3) | async-done | bytes 524320 | tf_op jit(solution)/shard_map/all_to_all | solution.py:173
  122.8 0.0 copy-done.8
  122.8 0.8 copy-done.2
  123.6 2.5 %last.1 = bf16[2,128,128]{2,1,0:T(8,128)(2,1)} custom-call(bf16[16,128,128]{2,1,0:T(8,128)(2,1)} %copy-done.2, bf16[2,8,64,128]{3,2,1,0:T(8,128)(2,1)} %copy-done.5, bf16[2,8,64,128]{3,2,1,0:T(8,128)(2,1)} %copy-done.6, bf16[2,8,64,128]{3,2,1,0:T(8,128)(2,1)} %copy-done.7, bf16[2,8,64,128]{3,2,1,0:T(8,128)(2,1)} %copy-done.8), custom_call_target="tpu_custom_call" | custom-call | tf_op jit(solution)/shard_map/last/pallas_call | solution.py:174
  126.0 4.7 %all_to_all.25 = bf16[2,128,128]{2,1,0:T(8,128)(2,1)S(1)} all-to-all(bf16[2,128,128]{2,1,0:T(8,128)(2,1)} %last.1), channel_id=1, replica_groups=mesh['zl'=4,'y'=4,'x'=4,'zh'=4,'co'=2] {'co'}, dimensions={0} | all-to-all | bytes 131072 | tf_op jit(solution)/shard_map/all_to_all | solution.py:181
  130.7 3.5 %collective-permute-start.4 = (bf16[256,128]{1,0:T(8,128)(2,1)S(1)}, bf16[256,128]{1,0:T(8,128)(2,1)S(1)}, u32[]{:S(2)}, u32[]{:S(2)}) collective-permute-start(bf16[256,128]{1,0:T(8,128)(2,1)S(1)} %bitcast.18), channel_id=1, source_target_pairs={{0,0},{1,1},{2,32},{3,33},{4,64},{5,65},{6,96},{7,97},{8,128},{9,1... | collective-permute-start | bytes 196616 | tf_op jit(solution)/shard_map/ppermute | solution.py:182
  134.3 16.1 %collective-permute-done.4 = bf16[256,128]{1,0:T(8,128)(2,1)S(1)} collective-permute-done((bf16[256,128]{1,0:T(8,128)(2,1)S(1)}, bf16[256,128]{1,0:T(8,128)(2,1)S(1)}, u32[]{:S(2)}, u32[]{:S(2)}) %collective-permute-start.4) | collective-permute-done | bytes 65568 | tf_op jit(solution)/shard_map/ppermute | solution.py:182
  150.4 0.6 copy.9
  (12 shorter events, 0.1 us)
Async XLA Ops:
  2.6 7.2 %copy-start.11 = (bf16[2,64,128]{2,1,0:T(8,128)(2,1)S(1)}, bf16[2,64,128]{2,1,0:T(8,128)(2,1)}, u32[]{:S(2)}) copy-start(bf16[2,64,128]{2,1,0:T(8,128)(2,1)} %get-tuple-element.14) | copy-start | bytes 98308
  2.6 21.7 %all-to-all-start = ((bf16[16,3,64,128]{3,2,1,0:T(8,128)(2,1)}), bf16[16,3,64,128]{3,2,1,0:T(8,128)(2,1)S(1)}, u32[]{:S(2)}, u32[]{:S(2)}) async-start(bf16[16,3,64,128]{3,2,1,0:T(8,128)(2,1)} %get-tuple-element.15), calls=%async_computation | async-start | bytes 1572864 | tf_op jit(solution)/shard_map/all_to_all | solution.py:131
  9.8 9.4 %collective-permute-start = (bf16[2,64,128]{2,1,0:T(8,128)(2,1)S(1)}, bf16[2,64,128]{2,1,0:T(8,128)(2,1)S(1)}, u32[]{:S(2)}, u32[]{:S(2)}) collective-permute-start(bf16[2,64,128]{2,1,0:T(8,128)(2,1)S(1)} %copy-done.11), channel_id=1, source_target_pairs={{0,0},{1,1},{2,32},{3,33},{4,64},{5,65},{6,96},{7,97},{8,128},{9,1... | collective-permute-start | bytes 98312 | tf_op jit(solution)/shard_map/ppermute | solution.py:130
  24.3 0.9 copy-start
  27.3 8.3 %copy-start.9 = (bf16[2,4,64,128]{3,2,1,0:T(8,128)(2,1)S(1)}, bf16[2,4,64,128]{3,2,1,0:T(8,128)(2,1)}, u32[]{:S(2)}) copy-start(bf16[2,4,64,128]{3,2,1,0:T(8,128)(2,1)} %get-tuple-element.17) | copy-start | bytes 393220
  27.3 44.4 %all-to-all-start.1 = ((bf16[4,2,4,64,128]{4,3,2,1,0:T(8,128)(2,1)}), bf16[4,2,4,64,128]{4,3,2,1,0:T(8,128)(2,1)S(1)}, u32[]{:S(2)}, u32[]{:S(2)}) async-start(bf16[4,2,4,64,128]{4,3,2,1,0:T(8,128)(2,1)} %get-tuple-element.19), calls=%async_computation.1 | async-start | bytes 1048576 | tf_op jit(solution)/shard_map/all_to_all | solution.py:140
  33.0 0.7 copy-start.10
  71.7 0.8 copy-start.3
  74.8 9.1 %copy-start.1 = (bf16[24,64,128]{2,1,0:T(8,128)(2,1)S(1)}, bf16[24,64,128]{2,1,0:T(8,128)(2,1)}, u32[]{:S(2)}) copy-start(bf16[24,64,128]{2,1,0:T(8,128)(2,1)} %all-gather.2) | copy-start | bytes 1179652
  74.8 24.1 %all-to-all-start.2 = ((bf16[16,128,128]{2,1,0:T(8,128)(2,1)}), bf16[16,128,128]{2,1,0:T(8,128)(2,1)S(1)}, u32[]{:S(2)}, u32[]{:S(2)}) async-start(bf16[16,128,128]{2,1,0:T(8,128)(2,1)} %product.1), calls=%async_computation.2 | async-start | bytes 1048576 | tf_op jit(solution)/shard_map/all_to_all | solution.py:161
  84.0 24.4 %copy-start.5 = (bf16[2,8,64,128]{3,2,1,0:T(8,128)(2,1)}, bf16[2,8,64,128]{3,2,1,0:T(8,128)(2,1)S(1)}, u32[]{:S(2)}) copy-start(bf16[2,8,64,128]{3,2,1,0:T(8,128)(2,1)S(1)} %slice.22.slabs_and_out_0_) | copy-start | bytes 786436
  84.0 15.0 %collective-permute-start.1 = (bf16[2,8,64,128]{3,2,1,0:T(8,128)(2,1)S(1)}, bf16[2,8,64,128]{3,2,1,0:T(8,128)(2,1)S(1)}, u32[]{:S(2)}, u32[]{:S(2)}) collective-permute-start(bf16[2,8,64,128]{3,2,1,0:T(8,128)(2,1)S(1)} %slice.22.slabs_and_out_0_), channel_id=1, source_target_pairs={{0,8},{8,16},{16,24},{24,0},{1,9},{9,17},{17,25},{25,1},{2,10},{10... | collective-permute-start | bytes 786440 | tf_op jit(solution)/shard_map/ppermute | solution.py:164
  87.8 11.1 %collective-permute-start.2 = (bf16[2,8,64,128]{3,2,1,0:T(8,128)(2,1)S(1)}, bf16[2,8,64,128]{3,2,1,0:T(8,128)(2,1)S(1)}, u32[]{:S(2)}, u32[]{:S(2)}) collective-permute-start(bf16[2,8,64,128]{3,2,1,0:T(8,128)(2,1)S(1)} %slice.22.slabs_and_out_0_), channel_id=1, source_target_pairs={{0,24},{8,0},{16,8},{24,16},{1,25},{9,1},{17,9},{25,17},{2,26},{10... | collective-permute-start | bytes 786440 | tf_op jit(solution)/shard_map/ppermute | solution.py:164
  98.9 2.8 %copy-start.6 = (bf16[2,8,64,128]{3,2,1,0:T(8,128)(2,1)}, bf16[2,8,64,128]{3,2,1,0:T(8,128)(2,1)S(1)}, u32[]{:S(2)}) copy-start(bf16[2,8,64,128]{3,2,1,0:T(8,128)(2,1)S(1)} %collective-permute-done.1.slabs_and_out_1_) | copy-start | bytes 786436
  98.9 2.8 %copy-start.7 = (bf16[2,8,64,128]{3,2,1,0:T(8,128)(2,1)}, bf16[2,8,64,128]{3,2,1,0:T(8,128)(2,1)S(1)}, u32[]{:S(2)}) copy-start(bf16[2,8,64,128]{3,2,1,0:T(8,128)(2,1)S(1)} %collective-permute-done.2.slabs_and_out_2_) | copy-start | bytes 786436
  98.9 0.8 copy-start.4
  101.7 21.0 %all-to-all-start.3 = ((bf16[16,128,128]{2,1,0:T(8,128)(2,1)}), bf16[16,128,128]{2,1,0:T(8,128)(2,1)S(1)}, u32[]{:S(2)}, u32[]{:S(2)}) async-start(bf16[16,128,128]{2,1,0:T(8,128)(2,1)} %total.1), calls=%async_computation.3 | async-start | bytes 1048576 | tf_op jit(solution)/shard_map/all_to_all | solution.py:173
  108.4 10.8 %collective-permute-start.3 = (bf16[2,8,64,128]{3,2,1,0:T(8,128)(2,1)S(1)}, bf16[2,8,64,128]{3,2,1,0:T(8,128)(2,1)S(1)}, u32[]{:S(2)}, u32[]{:S(2)}) collective-permute-start(bf16[2,8,64,128]{3,2,1,0:T(8,128)(2,1)S(1)} %slice.22.slabs_and_out_0_), channel_id=1, source_target_pairs={{0,16},{8,24},{16,0},{24,8},{1,17},{9,25},{17,1},{25,9},{2,18},{10... | collective-permute-start | bytes 786440 | tf_op jit(solution)/shard_map/ppermute | solution.py:164
  119.1 3.6 %copy-start.8 = (bf16[2,8,64,128]{3,2,1,0:T(8,128)(2,1)}, bf16[2,8,64,128]{3,2,1,0:T(8,128)(2,1)S(1)}, u32[]{:S(2)}) copy-start(bf16[2,8,64,128]{3,2,1,0:T(8,128)(2,1)S(1)} %collective-permute-done.3.slabs_and_out_3_) | copy-start | bytes 786436
  122.8 0.8 copy-start.2
  130.7 19.6 %collective-permute-start.4 = (bf16[256,128]{1,0:T(8,128)(2,1)S(1)}, bf16[256,128]{1,0:T(8,128)(2,1)S(1)}, u32[]{:S(2)}, u32[]{:S(2)}) collective-permute-start(bf16[256,128]{1,0:T(8,128)(2,1)S(1)} %bitcast.18), channel_id=1, source_target_pairs={{0,0},{1,1},{2,32},{3,33},{4,64},{5,65},{6,96},{7,97},{8,128},{9,1... | collective-permute-start | bytes 196616 | tf_op jit(solution)/shard_map/ppermute | solution.py:182

commit v3 on v2

--- a/solution.py
+++ b/solution.py
@@ -56,11 +56,13 @@
 
 
 def choose_kernel(blocks, got, part_h, part_z):
+    place = lax.axis_index("zh") * 2 + lax.axis_index("co")
     for s in range(SECTIONS):
         x0 = owner_col(blocks, s) // 8
         y0 = lax.rem(owner_row(blocks, s), 4)
+        owned = jnp.where(lax.rem(owner_col(blocks, s), 8) == place, 1, 0)
         for i in range(4):
-            part_h[s, i] = got[4 * i + x0, 0]
+            part_h[s, i] = got[4 * i + x0, 0] * lane_mask(owned, owned)
             block = got[4 * y0 + i, 1 + s]
             for copy in range(4):
                 part_z[copy, s, i] = block
@@ -68,11 +70,12 @@
 
 def product_kernel(blocks, pair, all_z, out):
     z0 = [owner_row(blocks, s) // 4 for s in range(SECTIONS)]
+    zh0 = [lax.rem(owner_col(blocks, s) // 2, 4) for s in range(SECTIONS)]
     right = [
         jnp.concatenate([all_z[z0[s], s, x] for s in range(SECTIONS)], axis=0) for x in range(4)
     ]
     for y in range(4):
-        left = jnp.concatenate([pair[s, y] for s in range(SECTIONS)], axis=0)
+        left = jnp.concatenate([pair[s, zh0[s], y] for s in range(SECTIONS)], axis=0)
         for x in range(4):
             out[4 * y + x] = lax.dot_general(
                 left, right[x], (((0,), (0,)), ((), ())), preferred_element_type=jnp.float32
@@ -88,17 +91,18 @@
         copies[i] = total
 
 
-def last_kernel(y_col, *slabs_and_out):
-    slabs, out = slabs_and_out[:-1], slabs_and_out[-1]
-    for core in range(2):
+def last_kernel(y_col, own, two, one, three, swapped, out):
+    co = lax.axis_index("co")
+    here = (own.at[co], two.at[co], one, three)
+    there = (own.at[1 - co], two.at[1 - co], swapped.at[0], swapped.at[1])
+    for core, slabs in ((co, here), (1 - co, there)):
         total = jnp.zeros((LANES, LANES), jnp.float32)
-        for back, slab in zip((0, 1, 3, 2), slabs):
+        for back, slab in zip((0, 2, 1, 3), slabs):
             x = lax.rem(lax.axis_index("x") + 4 - back, 4)
             for zh in range(4):
-                right = jnp.concatenate([slab[core, 2 * zh + i] for i in range(2)], axis=0)
                 total = total + lax.dot_general(
                     y_col[4 * x + zh],
-                    right,
+                    slab[zh],
                     (((0,), (0,)), ((), ())),
                     preferred_element_type=jnp.float32,
                 )
@@ -139,18 +143,11 @@
     )(blocks, got)
     all_z = lax.all_to_all(part_z, "zl", 0, 0, tiled=True)
     core = lax.axis_index("co")
-    first = jnp.where(core == 0, blocks[0, 0], blocks[1, 0])
-    owner_core = lax.shift_right_logical(first, 5) & 1
-    owner_zh = lax.shift_right_logical(first, 6) & 3
     pair_h = lax.all_gather(part_h, "co", axis=0)
-    mine_h = lax.dynamic_slice(
-        pair_h, (owner_core, core, 0, 0, 0), (1, 1) + part_h.shape[1:]
-    )
-    across = lax.all_gather(jnp.concatenate([mine_h[0, 0], slab], axis=0), "zh", axis=0)
-    from_owner = lax.dynamic_index_in_dim(across[:, :4], owner_zh, 0, keepdims=False)
-    pair = lax.all_gather(
-        jnp.concatenate([from_owner, across[:, 4:].reshape(8, BS, LANES)], axis=0), "co", axis=0
-    )
+    mine_h = lax.dynamic_index_in_dim(pair_h, core, 1, keepdims=False)
+    mine_h = mine_h[0] + mine_h[1]
+    across = lax.all_gather(jnp.concatenate([mine_h, slab], axis=0), "zh", axis=0)
+    pair = lax.all_gather(across, "co", axis=0)
     partial = pl.pallas_call(
         product_kernel,
         out_shape=shape(16, LANES, LANES),
@@ -159,10 +156,14 @@
         name="product",
     )(blocks, pair, all_z)
     partial = lax.all_to_all(partial, PLANE, 0, 0, tiled=True)
-    slabs = [pair[:, 4:]]
-    for back in (1, 3, 2):
-        slabs.append(lax.ppermute(slabs[0], "x", [(x, (x + back) % 4) for x in range(4)]))
-    slabs[1], slabs[2], partial = lax.optimization_barrier((slabs[1], slabs[2], partial))
+    own = across[:, 4:].reshape(4, LANES, LANES)
+    both = pair[:, :, 4:].reshape(2, 4, LANES, LANES)
+    one, three = [
+        lax.ppermute(own, "x", [(x, (x + back) % 4) for x in range(4)]) for back in (1, 3)
+    ]
+    two = lax.ppermute(both, "x", [(x, (x + 2) % 4) for x in range(4)])
+    one, three, partial = lax.optimization_barrier((one, three, partial))
+    swapped = lax.ppermute(jnp.stack([one, three]), "co", [(0, 1), (1, 0)])
     copies = pl.pallas_call(
         total_kernel,
         out_shape=shape(16, LANES, LANES),
@@ -174,10 +175,10 @@
     halves = pl.pallas_call(
         last_kernel,
         out_shape=shape(2, LANES, LANES),
-        in_specs=[VMEM] * 5,
+        in_specs=[VMEM] * 6,
         out_specs=VMEM,
         name="last",
-    )(y_col, *slabs)
+    )(y_col, both, two, one, three, swapped)
     k_block = lax.all_to_all(halves, "co", 0, 0, tiled=True)
     return lax.ppermute(k_block.reshape(-1, LANES), ALL, swapped_pairs())
 

time: 152 us -> 148 us (0.974)
  blocking collectives: 40.7 us -> 47.4 us
  waiting for transfers between devices: 43.2 us -> 37.3 us
  starting transfers between devices: 48.8 us -> 46 us
    all_gather x2, blocking collectives: 34 us -> 40.7 us  [the longest x1 38.2 us: per_device(): lax.all_gather(jnp.concatenate([mine_h, slab], axis=0), 'zh', axis=0)]
    all_to_all x1, starting transfers between devices: 9.08 us -> 5.15 us  [per_device(): partial = lax.all_to_all(partial, PLANE, 0, 0, tiled=True)]
    ppermute x3 -> x4, waiting for transfers between devices: 15.3 us -> 11.4 us  [the longest x2 6.14 us: per_device(): lax.ppermute(own, 'x', [(x, (x + back) % 4) for x in range(4)])]
    ppermute x3 -> x4, starting transfers between devices: 10.4 us -> 11.4 us  [the longest x2 6.96 us: per_device(): lax.ppermute(own, 'x', [(x, (x + back) % 4) for x in range(4)])]
    unnamed x25 -> x23, local copies, waits for them, and re-layouts: 4.67 us -> 3.97 us
  transfers between devices with their start and end apart: 9 -> 10, of which waited for: 6 -> 7; matrix products, arithmetic and copies ran while one was open for 0% -> 1% of each run, Pallas kernels for 0% -> 0%
where the time goes in v3:
time: 148 us
  blocking collectives  47.4 us (32%)
  starting transfers between devices  46 us (31%)
  waiting for transfers between devices  37.3 us (25%)
  Pallas kernels  11.7 us (8%)
  local copies, waits for them, and re-layouts  4.95 us (3%)
    all_gather x1, blocking collectives, per_device(): lax.all_gather(jnp.concatenate([mine_h, slab], axis=0), 'zh', axis=0)  38.2 us
    ppermute x1, waiting for transfers between devices, per_device(): return lax.ppermute(k_block.reshape(-1, LANES), ALL, swapped_pairs())  15.4 us
    all_to_all x1, starting transfers between devices, per_device(): got = lax.all_to_all(packed, PLANE, 0, 0, tiled=True)  7.17 us
    ppermute x2, starting transfers between devices, per_device(): lax.ppermute(own, 'x', [(x, (x + back) % 4) for x in range(4)])  6.96 us
    all_to_all x1, starting transfers between devices, per_device(): y_col = lax.all_to_all(copies, ROW, 0, 0, tiled=True)  6.62 us
    ppermute x1, starting transfers between devices, per_device(): slab = lax.ppermute(slab, ALL, swapped_pairs())  6.26 us
    ppermute x2, waiting for transfers between devices, per_device(): lax.ppermute(own, 'x', [(x, (x + back) % 4) for x in range(4)])  6.14 us
    all_to_all x1, starting transfers between devices, per_device(): all_z = lax.all_to_all(part_z, 'zl', 0, 0, tiled=True)  5.68 us
  transfers between devices with their start and end apart: 10, of which 7 were waited for; matrix products, arithmetic and copies ran while one was open for 1% of the time, Pallas kernels for 0%

profile of v3, /device:TPU:64, one launch (start us, length us, event | category | flops | bytes accessed | tf_op | source)
XLA Modules:
  0.0 147.5 jit_solution(14583454302254943308)
XLA Ops:
  0.0 2.6 %pick.1 = (bf16[16,3,64,128]{3,2,1,0:T(8,128)(2,1)}, bf16[2,64,128]{2,1,0:T(8,128)(2,1)}) custom-call(s32[2,16]{1,0:T(2,128)} %blocks.5, s32[2,32]{1,0:T(2,128)} %mask_h.1, s32[2,64]{1,0:T(2,128)} %bitcast.23, s32[2,2]{1,0:T(2,128)} %mask_slab.1, bf16[128,2048]{1,0:T(8,128)(2,1)} %h.1, bf16[4096,128]{1,0:T(8,128)(2,1)} %z.1, bf16[128,128]{1,0:T(8,128)(2,1)} %slab.1), custom_call_target="tpu_custom_call" | custom-call | tf_op jit(solution)/shard_map/pick/pallas_call | solution.py:126
  2.6 0.0 copy-start.10
  2.7 7.2 %all-to-all-start = ((bf16[16,3,64,128]{3,2,1,0:T(8,128)(2,1)}), bf16[16,3,64,128]{3,2,1,0:T(8,128)(2,1)S(1)}, u32[]{:S(2)}, u32[]{:S(2)}) async-start(bf16[16,3,64,128]{3,2,1,0:T(8,128)(2,1)} %get-tuple-element.15), calls=%async_computation | async-start | bytes 1572864 | tf_op jit(solution)/shard_map/all_to_all | solution.py:135
  9.8 0.0 copy-done.10
  9.8 6.3 %collective-permute-start = (bf16[2,64,128]{2,1,0:T(8,128)(2,1)S(1)}, bf16[2,64,128]{2,1,0:T(8,128)(2,1)S(1)}, u32[]{:S(2)}, u32[]{:S(2)}) collective-permute-start(bf16[2,64,128]{2,1,0:T(8,128)(2,1)S(1)} %copy-done.10), channel_id=1, source_target_pairs={{0,0},{1,1},{2,32},{3,33},{4,64},{5,65},{6,96},{7,97},{8,128},{9,1... | collective-permute-start | bytes 98312 | tf_op jit(solution)/shard_map/ppermute | solution.py:134
  16.1 3.1 %collective-permute-done = bf16[2,64,128]{2,1,0:T(8,128)(2,1)S(1)} collective-permute-done((bf16[2,64,128]{2,1,0:T(8,128)(2,1)S(1)}, bf16[2,64,128]{2,1,0:T(8,128)(2,1)S(1)}, u32[]{:S(2)}, u32[]{:S(2)}) %collective-permute-start) | collective-permute-done | bytes 32800 | tf_op jit(solution)/shard_map/ppermute | solution.py:134
  19.2 5.1 %all-to-all-done.got = bf16[16,3,64,128]{3,2,1,0:T(8,128)(2,1)S(1)} async-done(((bf16[16,3,64,128]{3,2,1,0:T(8,128)(2,1)}), bf16[16,3,64,128]{3,2,1,0:T(8,128)(2,1)S(1)}, u32[]{:S(2)}, u32[]{:S(2)}) %all-to-all-start) | async-done | bytes 786464 | tf_op jit(solution)/shard_map/all_to_all | solution.py:135
  24.3 0.0 copy-start
  24.3 0.9 copy-done
  25.2 2.1 %choose.1 = (bf16[2,4,64,128]{3,2,1,0:T(8,128)(2,1)}, bf16[4,2,4,64,128]{4,3,2,1,0:T(8,128)(2,1)}) custom-call(s32[2,16]{1,0:T(2,128)} %blocks.5, bf16[16,3,64,128]{3,2,1,0:T(8,128)(2,1)} %copy-done), custom_call_target="tpu_custom_call" | custom-call | tf_op jit(solution)/shard_map/choose/pallas_call | solution.py:137
  27.3 0.0 copy-start.9
  27.3 5.7 %all-to-all-start.1 = ((bf16[4,2,4,64,128]{4,3,2,1,0:T(8,128)(2,1)}), bf16[4,2,4,64,128]{4,3,2,1,0:T(8,128)(2,1)S(1)}, u32[]{:S(2)}, u32[]{:S(2)}) async-start(bf16[4,2,4,64,128]{4,3,2,1,0:T(8,128)(2,1)} %get-tuple-element.19), calls=%async_computation.1 | async-start | bytes 1048576 | tf_op jit(solution)/shard_map/all_to_all | solution.py:144
  33.0 0.0 copy-done.9
  33.0 2.0 %all-gather = bf16[4,4,64,128]{3,2,1,0:T(8,128)(2,1)S(1)} all-gather(bf16[2,4,64,128]{3,2,1,0:T(8,128)(2,1)S(1)} %copy-done.9), channel_id=2, replica_groups=mesh['zl'=4,'y'=4,'x'=4,'zh'=4,'co'=2] {'co'}, dimensions={0}, use_global_device_ids=true | all-gather | bytes 393216 | tf_op jit(solution)/shard_map/all_gather | solution.py:146
  35.0 38.2 %all-gather.1 = bf16[24,64,128]{2,1,0:T(8,128)(2,1)S(1)} all-gather(bf16[6,64,128]{2,1,0:T(8,128)(2,1)S(1)} %pad_maximum_fusion.1), channel_id=3, replica_groups=mesh['zl'=4,'y'=4,'x'=4,'zh'=4,'co'=2] {'zh'}, dimensions={0}, use_global_device_ids=true | all-gather | bytes 491520 | tf_op jit(solution)/shard_map/all_gather | solution.py:149
  73.3 2.5 %all-gather.2 = bf16[8,6,64,128]{3,2,1,0:T(8,128)(2,1)} all-gather(bf16[4,6,64,128]{3,2,1,0:T(8,128)(2,1)S(1)} %bitcast.13), channel_id=4, replica_groups=mesh['zl'=4,'y'=4,'x'=4,'zh'=4,'co'=2] {'co'}, dimensions={0}, use_global_device_ids=true | all-gather | bytes 1179648 | tf_op jit(solution)/shard_map/all_gather | solution.py:150
  75.8 0.0 all-to-all-done.1.all_z
  75.8 0.0 copy-start.1
  75.8 0.8 copy-done.1
  76.6 2.5 %product.1 = bf16[16,128,128]{2,1,0:T(8,128)(2,1)} custom-call(s32[2,16]{1,0:T(2,128)} %blocks.5, bf16[2,4,6,64,128]{4,3,2,1,0:T(8,128)(2,1)} %bitcast.11, bf16[4,2,4,64,128]{4,3,2,1,0:T(8,128)(2,1)} %copy-done.1), custom_call_target="tpu_custom_call" | custom-call | tf_op jit(solution)/shard_map/product/pallas_call | solution.py:151
  79.1 5.1 %all-to-all-start.2 = ((bf16[16,128,128]{2,1,0:T(8,128)(2,1)}), bf16[16,128,128]{2,1,0:T(8,128)(2,1)S(1)}, u32[]{:S(2)}, u32[]{:S(2)}) async-start(bf16[16,128,128]{2,1,0:T(8,128)(2,1)} %product.1), calls=%async_computation.2 | async-start | bytes 1048576 | tf_op jit(solution)/shard_map/all_to_all | solution.py:158
  84.2 5.0 %collective-permute-start.2 = (bf16[4,128,128]{2,1,0:T(8,128)(2,1)S(1)}, bf16[4,128,128]{2,1,0:T(8,128)(2,1)S(1)}, u32[]{:S(2)}, u32[]{:S(2)}) collective-permute-start(bf16[4,128,128]{2,1,0:T(8,128)(2,1)S(1)} %bitcast.20), channel_id=1, source_target_pairs={{0,24},{8,0},{16,8},{24,16},{1,25},{9,1},{17,9},{25,17},{2,26},{10... | collective-permute-start | bytes 393224 | tf_op jit(solution)/shard_map/ppermute | solution.py:162
  89.3 1.9 %collective-permute-start.1 = (bf16[4,128,128]{2,1,0:T(8,128)(2,1)S(1)}, bf16[4,128,128]{2,1,0:T(8,128)(2,1)S(1)}, u32[]{:S(2)}, u32[]{:S(2)}) collective-permute-start(bf16[4,128,128]{2,1,0:T(8,128)(2,1)S(1)} %bitcast.21), channel_id=1, source_target_pairs={{0,8},{8,16},{16,24},{24,0},{1,9},{9,17},{17,25},{25,1},{2,10},{10... | collective-permute-start | bytes 393224 | tf_op jit(solution)/shard_map/ppermute | solution.py:162
  91.2 4.0 %collective-permute-done.2.three = bf16[4,128,128]{2,1,0:T(8,128)(2,1)S(1)} collective-permute-done((bf16[4,128,128]{2,1,0:T(8,128)(2,1)S(1)}, bf16[4,128,128]{2,1,0:T(8,128)(2,1)S(1)}, u32[]{:S(2)}, u32[]{:S(2)}) %collective-permute-start.2) | collective-permute-done | bytes 131104 | tf_op jit(solution)/shard_map/ppermute | solution.py:162
  95.2 0.0 copy-start.5
  95.2 2.1 %collective-permute-done.1.one = bf16[4,128,128]{2,1,0:T(8,128)(2,1)S(1)} collective-permute-done((bf16[4,128,128]{2,1,0:T(8,128)(2,1)S(1)}, bf16[4,128,128]{2,1,0:T(8,128)(2,1)S(1)}, u32[]{:S(2)}, u32[]{:S(2)}) %collective-permute-start.1) | collective-permute-done | bytes 131104 | tf_op jit(solution)/shard_map/ppermute | solution.py:162
  97.4 0.0 all-to-all-done.2.parts
  97.4 0.8 copy-done.3
  98.2 2.0 %total.1 = bf16[16,128,128]{2,1,0:T(8,128)(2,1)} custom-call(bf16[16,128,128]{2,1,0:T(8,128)(2,1)} %copy-done.3), custom_call_target="tpu_custom_call" | custom-call | tf_op jit(solution)/shard_map/total/pallas_call | solution.py:167
  100.2 6.6 %all-to-all-start.3 = ((bf16[16,128,128]{2,1,0:T(8,128)(2,1)}), bf16[16,128,128]{2,1,0:T(8,128)(2,1)S(1)}, u32[]{:S(2)}, u32[]{:S(2)}) async-start(bf16[16,128,128]{2,1,0:T(8,128)(2,1)} %total.1), calls=%async_computation.3 | async-start | bytes 1048576 | tf_op jit(solution)/shard_map/all_to_all | solution.py:174
  106.8 1.0 slice.19
  107.8 0.0 copy-start.4
  107.8 2.5 %collective-permute-start.3 = (bf16[2,4,128,128]{3,2,1,0:T(8,128)(2,1)S(1)}, bf16[2,4,128,128]{3,2,1,0:T(8,128)(2,1)S(1)}, u32[]{:S(2)}, u32[]{:S(2)}) collective-permute-start(bf16[2,4,128,128]{3,2,1,0:T(8,128)(2,1)S(1)} %bitcast.15), channel_id=1, source_target_pairs={{0,16},{8,24},{16,0},{24,8},{1,17},{9,25},{17,1},{25,9},{2,18},{10... | collective-permute-start | bytes 786440 | tf_op jit(solution)/shard_map/ppermute | solution.py:164
  110.2 0.0 copy-done.5
  110.3 0.0 copy-done.6
  110.3 0.0 copy-done.4
  110.3 1.9 %collective-permute-start.4 = (bf16[2,4,128,128]{3,2,1,0:T(8,128)(2,1)S(1)}, bf16[2,4,128,128]{3,2,1,0:T(8,128)(2,1)S(1)}, u32[]{:S(2)}, u32[]{:S(2)}) collective-permute-start(bf16[2,4,128,128]{3,2,1,0:T(8,128)(2,1)S(1)} %pad_maximum_fusion), channel_id=1, source_target_pairs={{0,1},{1,0},{2,3},{3,2},{4,5},{5,4},{6,7},{7,6},{8,9},{9,8},{10,11... | collective-permute-start | bytes 786440 | tf_op jit(solution)/shard_map/ppermute | solution.py:166
  112.2 5.3 %collective-permute-done.3.two = bf16[2,4,128,128]{3,2,1,0:T(8,128)(2,1)S(1)} collective-permute-done((bf16[2,4,128,128]{3,2,1,0:T(8,128)(2,1)S(1)}, bf16[2,4,128,128]{3,2,1,0:T(8,128)(2,1)S(1)}, u32[]{:S(2)}, u32[]{:S(2)}) %collective-permute-start.3) | collective-permute-done | bytes 262176 | tf_op jit(solution)/shard_map/ppermute | solution.py:164
  117.5 0.0 collective-permute-done.4.swapped
  117.5 2.2 %all-to-all-done.3.y_col = bf16[16,128,128]{2,1,0:T(8,128)(2,1)S(1)} async-done(((bf16[16,128,128]{2,1,0:T(8,128)(2,1)}), bf16[16,128,128]{2,1,0:T(8,128)(2,1)S(1)}, u32[]{:S(2)}, u32[]{:S(2)}) %all-to-all-start.3) | async-done | bytes 524320 | tf_op jit(solution)/shard_map/all_to_all | solution.py:174
  119.8 0.0 copy-done.7
  119.8 0.0 copy-done.8
  119.8 0.8 copy-done.2
  120.6 2.5 %last.1 = bf16[2,128,128]{2,1,0:T(8,128)(2,1)} custom-call(bf16[16,128,128]{2,1,0:T(8,128)(2,1)} %copy-done.2, bf16[2,4,128,128]{3,2,1,0:T(8,128)(2,1)} %bitcast.16, bf16[2,4,128,128]{3,2,1,0:T(8,128)(2,1)} %copy-done.7, bf16[4,128,128]{2,1,0:T(8,128)(2,1)} %copy-done.6, bf16[4,128,128]{2,1,0:T(8,128)(2,1)} %copy-done.5, bf16[2,4,128,128]{3,2,1,0:T(8,128)(2,1)} %copy-done.8), custom_call_target="tpu_custom_call" | custom-call | tf_op jit(solution)/shard_map/last/pallas_call | solution.py:175
  123.0 4.7 %all_to_all.25 = bf16[2,128,128]{2,1,0:T(8,128)(2,1)S(1)} all-to-all(bf16[2,128,128]{2,1,0:T(8,128)(2,1)} %last.1), channel_id=1, replica_groups=mesh['zl'=4,'y'=4,'x'=4,'zh'=4,'co'=2] {'co'}, dimensions={0} | all-to-all | bytes 131072 | tf_op jit(solution)/shard_map/all_to_all | solution.py:182
  127.7 3.7 %collective-permute-start.5 = (bf16[256,128]{1,0:T(8,128)(2,1)S(1)}, bf16[256,128]{1,0:T(8,128)(2,1)S(1)}, u32[]{:S(2)}, u32[]{:S(2)}) collective-permute-start(bf16[256,128]{1,0:T(8,128)(2,1)S(1)} %bitcast.22), channel_id=1, source_target_pairs={{0,0},{1,1},{2,32},{3,33},{4,64},{5,65},{6,96},{7,97},{8,128},{9,1... | collective-permute-start | bytes 196616 | tf_op jit(solution)/shard_map/ppermute | solution.py:183
  131.5 15.4 %collective-permute-done.5 = bf16[256,128]{1,0:T(8,128)(2,1)S(1)} collective-permute-done((bf16[256,128]{1,0:T(8,128)(2,1)S(1)}, bf16[256,128]{1,0:T(8,128)(2,1)S(1)}, u32[]{:S(2)}, u32[]{:S(2)}) %collective-permute-start.5) | collective-permute-done | bytes 65568 | tf_op jit(solution)/shard_map/ppermute | solution.py:183
  146.9 0.6 copy.9
  (9 shorter events, 0.1 us)
Async XLA Ops:
  2.6 7.2 %copy-start.10 = (bf16[2,64,128]{2,1,0:T(8,128)(2,1)S(1)}, bf16[2,64,128]{2,1,0:T(8,128)(2,1)}, u32[]{:S(2)}) copy-start(bf16[2,64,128]{2,1,0:T(8,128)(2,1)} %get-tuple-element.14) | copy-start | bytes 98308
  2.7 21.7 %all-to-all-start = ((bf16[16,3,64,128]{3,2,1,0:T(8,128)(2,1)}), bf16[16,3,64,128]{3,2,1,0:T(8,128)(2,1)S(1)}, u32[]{:S(2)}, u32[]{:S(2)}) async-start(bf16[16,3,64,128]{3,2,1,0:T(8,128)(2,1)} %get-tuple-element.15), calls=%async_computation | async-start | bytes 1572864 | tf_op jit(solution)/shard_map/all_to_all | solution.py:135
  9.8 9.4 %collective-permute-start = (bf16[2,64,128]{2,1,0:T(8,128)(2,1)S(1)}, bf16[2,64,128]{2,1,0:T(8,128)(2,1)S(1)}, u32[]{:S(2)}, u32[]{:S(2)}) collective-permute-start(bf16[2,64,128]{2,1,0:T(8,128)(2,1)S(1)} %copy-done.10), channel_id=1, source_target_pairs={{0,0},{1,1},{2,32},{3,33},{4,64},{5,65},{6,96},{7,97},{8,128},{9,1... | collective-permute-start | bytes 98312 | tf_op jit(solution)/shard_map/ppermute | solution.py:134
  24.3 0.9 copy-start
  27.3 5.7 %copy-start.9 = (bf16[2,4,64,128]{3,2,1,0:T(8,128)(2,1)S(1)}, bf16[2,4,64,128]{3,2,1,0:T(8,128)(2,1)}, u32[]{:S(2)}) copy-start(bf16[2,4,64,128]{3,2,1,0:T(8,128)(2,1)} %get-tuple-element.17) | copy-start | bytes 393220
  27.3 48.4 %all-to-all-start.1 = ((bf16[4,2,4,64,128]{4,3,2,1,0:T(8,128)(2,1)}), bf16[4,2,4,64,128]{4,3,2,1,0:T(8,128)(2,1)S(1)}, u32[]{:S(2)}, u32[]{:S(2)}) async-start(bf16[4,2,4,64,128]{4,3,2,1,0:T(8,128)(2,1)} %get-tuple-element.19), calls=%async_computation.1 | async-start | bytes 1048576 | tf_op jit(solution)/shard_map/all_to_all | solution.py:144
  75.8 0.8 copy-start.1
  79.1 18.3 %all-to-all-start.2 = ((bf16[16,128,128]{2,1,0:T(8,128)(2,1)}), bf16[16,128,128]{2,1,0:T(8,128)(2,1)S(1)}, u32[]{:S(2)}, u32[]{:S(2)}) async-start(bf16[16,128,128]{2,1,0:T(8,128)(2,1)} %product.1), calls=%async_computation.2 | async-start | bytes 1048576 | tf_op jit(solution)/shard_map/all_to_all | solution.py:158
  84.2 11.0 %collective-permute-start.2 = (bf16[4,128,128]{2,1,0:T(8,128)(2,1)S(1)}, bf16[4,128,128]{2,1,0:T(8,128)(2,1)S(1)}, u32[]{:S(2)}, u32[]{:S(2)}) collective-permute-start(bf16[4,128,128]{2,1,0:T(8,128)(2,1)S(1)} %bitcast.20), channel_id=1, source_target_pairs={{0,24},{8,0},{16,8},{24,16},{1,25},{9,1},{17,9},{25,17},{2,26},{10... | collective-permute-start | bytes 393224 | tf_op jit(solution)/shard_map/ppermute | solution.py:162
  89.3 8.1 %collective-permute-start.1 = (bf16[4,128,128]{2,1,0:T(8,128)(2,1)S(1)}, bf16[4,128,128]{2,1,0:T(8,128)(2,1)S(1)}, u32[]{:S(2)}, u32[]{:S(2)}) collective-permute-start(bf16[4,128,128]{2,1,0:T(8,128)(2,1)S(1)} %bitcast.21), channel_id=1, source_target_pairs={{0,8},{8,16},{16,24},{24,0},{1,9},{9,17},{17,25},{25,1},{2,10},{10... | collective-permute-start | bytes 393224 | tf_op jit(solution)/shard_map/ppermute | solution.py:162
  95.2 15.0 %copy-start.5 = (bf16[4,128,128]{2,1,0:T(8,128)(2,1)}, bf16[4,128,128]{2,1,0:T(8,128)(2,1)S(1)}, u32[]{:S(2)}) copy-start(bf16[4,128,128]{2,1,0:T(8,128)(2,1)S(1)} %collective-permute-done.2.three) | copy-start | bytes 393220
  97.3 12.9 %copy-start.6 = (bf16[4,128,128]{2,1,0:T(8,128)(2,1)}, bf16[4,128,128]{2,1,0:T(8,128)(2,1)S(1)}, u32[]{:S(2)}) copy-start(bf16[4,128,128]{2,1,0:T(8,128)(2,1)S(1)} %collective-permute-done.1.one) | copy-start | bytes 393220
  97.4 0.8 copy-start.3
  100.2 19.6 %all-to-all-start.3 = ((bf16[16,128,128]{2,1,0:T(8,128)(2,1)}), bf16[16,128,128]{2,1,0:T(8,128)(2,1)S(1)}, u32[]{:S(2)}, u32[]{:S(2)}) async-start(bf16[16,128,128]{2,1,0:T(8,128)(2,1)} %total.1), calls=%async_computation.3 | async-start | bytes 1048576 | tf_op jit(solution)/shard_map/all_to_all | solution.py:174
  107.8 2.6 %copy-start.4 = (bf16[2,4,2,64,128]{4,3,2,1,0:T(8,128)(2,1)}, bf16[2,4,2,64,128]{4,3,2,1,0:T(8,128)(2,1)S(1)}, u32[]{:S(2)}) copy-start(bf16[2,4,2,64,128]{4,3,2,1,0:T(8,128)(2,1)S(1)} %slice.19) | copy-start | bytes 786436
  107.8 9.8 %collective-permute-start.3 = (bf16[2,4,128,128]{3,2,1,0:T(8,128)(2,1)S(1)}, bf16[2,4,128,128]{3,2,1,0:T(8,128)(2,1)S(1)}, u32[]{:S(2)}, u32[]{:S(2)}) collective-permute-start(bf16[2,4,128,128]{3,2,1,0:T(8,128)(2,1)S(1)} %bitcast.15), channel_id=1, source_target_pairs={{0,16},{8,24},{16,0},{24,8},{1,17},{9,25},{17,1},{25,9},{2,18},{10... | collective-permute-start | bytes 786440 | tf_op jit(solution)/shard_map/ppermute | solution.py:164
  110.3 7.2 %collective-permute-start.4 = (bf16[2,4,128,128]{3,2,1,0:T(8,128)(2,1)S(1)}, bf16[2,4,128,128]{3,2,1,0:T(8,128)(2,1)S(1)}, u32[]{:S(2)}, u32[]{:S(2)}) collective-permute-start(bf16[2,4,128,128]{3,2,1,0:T(8,128)(2,1)S(1)} %pad_maximum_fusion), channel_id=1, source_target_pairs={{0,1},{1,0},{2,3},{3,2},{4,5},{5,4},{6,7},{7,6},{8,9},{9,8},{10,11... | collective-permute-start | bytes 786440 | tf_op jit(solution)/shard_map/ppermute | solution.py:166
  117.5 2.2 %copy-start.7 = (bf16[2,4,128,128]{3,2,1,0:T(8,128)(2,1)}, bf16[2,4,128,128]{3,2,1,0:T(8,128)(2,1)S(1)}, u32[]{:S(2)}) copy-start(bf16[2,4,128,128]{3,2,1,0:T(8,128)(2,1)S(1)} %collective-permute-done.3.two) | copy-start | bytes 786436
  117.5 2.2 %copy-start.8 = (bf16[2,4,128,128]{3,2,1,0:T(8,128)(2,1)}, bf16[2,4,128,128]{3,2,1,0:T(8,128)(2,1)S(1)}, u32[]{:S(2)}) copy-start(bf16[2,4,128,128]{3,2,1,0:T(8,128)(2,1)S(1)} %collective-permute-done.4.swapped) | copy-start | bytes 786436
  119.8 0.8 copy-start.2
  127.7 19.2 %collective-permute-start.5 = (bf16[256,128]{1,0:T(8,128)(2,1)S(1)}, bf16[256,128]{1,0:T(8,128)(2,1)S(1)}, u32[]{:S(2)}, u32[]{:S(2)}) collective-permute-start(bf16[256,128]{1,0:T(8,128)(2,1)S(1)} %bitcast.22), channel_id=1, source_target_pairs={{0,0},{1,1},{2,32},{3,33},{4,64},{5,65},{6,96},{7,97},{8,128},{9,1... | collective-permute-start | bytes 196616 | tf_op jit(solution)/shard_map/ppermute | solution.py:183

commit v4 on v3

--- a/solution.py
+++ b/solution.py
@@ -55,19 +55,6 @@
         masked[i] = slab[at, :] * lane_mask(mask_slab[i, 0], mask_slab[i, 1])
 
 
-def choose_kernel(blocks, got, part_h, part_z):
-    place = lax.axis_index("zh") * 2 + lax.axis_index("co")
-    for s in range(SECTIONS):
-        x0 = owner_col(blocks, s) // 8
-        y0 = lax.rem(owner_row(blocks, s), 4)
-        owned = jnp.where(lax.rem(owner_col(blocks, s), 8) == place, 1, 0)
-        for i in range(4):
-            part_h[s, i] = got[4 * i + x0, 0] * lane_mask(owned, owned)
-            block = got[4 * y0 + i, 1 + s]
-            for copy in range(4):
-                part_z[copy, s, i] = block
-
-
 def product_kernel(blocks, pair, all_z, out):
     z0 = [owner_row(blocks, s) // 4 for s in range(SECTIONS)]
     zh0 = [lax.rem(owner_col(blocks, s) // 2, 4) for s in range(SECTIONS)]
@@ -80,15 +67,6 @@
             out[4 * y + x] = lax.dot_general(
                 left, right[x], (((0,), (0,)), ((), ())), preferred_element_type=jnp.float32
             ).astype(out.dtype)
-
-
-def total_kernel(parts, copies):
-    total = parts[0].astype(jnp.float32)
-    for i in range(1, parts.shape[0]):
-        total = total + parts[i].astype(jnp.float32)
-    total = total.astype(copies.dtype)
-    for i in range(copies.shape[0]):
-        copies[i] = total
 
 
 def last_kernel(y_col, own, two, one, three, swapped, out):
@@ -133,14 +111,29 @@
     )(blocks, mask_h, mask_panel.T, mask_slab, hamiltonian, z_panel, z_slab)
     slab = lax.ppermute(slab, ALL, swapped_pairs())
     got = lax.all_to_all(packed, PLANE, 0, 0, tiled=True)
-    slab, got = lax.optimization_barrier((slab, got))
-    part_h, part_z = pl.pallas_call(
-        choose_kernel,
-        out_shape=(shape(SECTIONS, 4, BS, LANES), shape(4, SECTIONS, 4, BS, LANES)),
-        in_specs=[SMEM, VMEM],
-        out_specs=(VMEM, VMEM),
-        name="choose",
-    )(blocks, got)
+    first = [blocks[s, 0] for s in range(SECTIONS)]
+    place = lax.axis_index("zh") * 2 + lax.axis_index("co")
+    outer = [lax.shift_right_logical(f, 8) for f in first]
+    inner = [lax.shift_right_logical(f, 6) & 3 for f in first]
+    owned = [
+        ((lax.shift_right_logical(f, 5) & 7) == place).astype(jnp.bfloat16) for f in first
+    ]
+    outer, inner, owned, got = lax.optimization_barrier((outer, inner, owned, got))
+    got = got.reshape(4, 4, 1 + SECTIONS, BS, LANES)
+    part_h = jnp.stack(
+        [
+            lax.dynamic_index_in_dim(got[:, :, 0], outer[s], 1, keepdims=False) * owned[s]
+            for s in range(SECTIONS)
+        ]
+    )
+    part_z = jnp.stack(
+        [
+            lax.dynamic_index_in_dim(got[:, :, 1 + s], inner[s], 0, keepdims=False)
+            for s in range(SECTIONS)
+        ]
+    )
+    part_z = jnp.broadcast_to(part_z, (4,) + part_z.shape)
+    slab, part_h, part_z = lax.optimization_barrier((slab, part_h, part_z))
     all_z = lax.all_to_all(part_z, "zl", 0, 0, tiled=True)
     core = lax.axis_index("co")
     pair_h = lax.all_gather(part_h, "co", axis=0)
@@ -164,13 +157,8 @@
     two = lax.ppermute(both, "x", [(x, (x + 2) % 4) for x in range(4)])
     one, three, partial = lax.optimization_barrier((one, three, partial))
     swapped = lax.ppermute(jnp.stack([one, three]), "co", [(0, 1), (1, 0)])
-    copies = pl.pallas_call(
-        total_kernel,
-        out_shape=shape(16, LANES, LANES),
-        in_specs=[VMEM],
-        out_specs=VMEM,
-        name="total",
-    )(partial)
+    total = jnp.sum(partial.astype(jnp.float32), axis=0).astype(jnp.bfloat16)
+    copies = jnp.broadcast_to(total, partial.shape)
     y_col = lax.all_to_all(copies, ROW, 0, 0, tiled=True)
     halves = pl.pallas_call(
         last_kernel,

time: 148 us -> 145 us (0.980)
  waiting for transfers between devices: 37.3 us -> 32.2 us
  Pallas kernels: 11.7 us -> 7.57 us
  between operations: 0.15 us -> 4.08 us
    pallas_call x2 -> x0, Pallas kernels: 4.09 us -> none  [the longest x1 2.12 us: per_device(): pl.pallas_call(choose_kernel, out_shape=(shape(SECTIONS, 4, BS, LANES), s...]
    ppermute x1, waiting for transfers between devices: 3.12 us -> 0.01 us  [per_device(): slab = lax.ppermute(slab, ALL, swapped_pairs())]
    all_to_all x1, waiting for transfers between devices: 5.1 us -> 3.13 us  [per_device(): got = lax.all_to_all(packed, PLANE, 0, 0, tiled=True)]
    broadcast_in_dim x0 -> x2, local copies, waits for them, and re-layouts: none -> 1.87 us  [the longest x1 0.94 us: per_device(): part_z = jnp.broadcast_to(part_z, (4,) + part_z.shape)]
    unnamed x23 -> x19, local copies, waits for them, and re-layouts: 3.97 us -> 2.92 us
  transfers between devices with their start and end apart: 10 -> 10, of which waited for: 7 -> 6; matrix products, arithmetic and copies ran while one was open for 1% -> 1% of each run, Pallas kernels for 0% -> 0%
where the time goes in v4:
time: 145 us; the launch traced here: 144 us
  blocking collectives  47.9 us (33%)
  starting transfers between devices  45.5 us (31%)
  waiting for transfers between devices  32.2 us (22%)
  Pallas kernels  7.57 us (5%)
  local copies, waits for them, and re-layouts  6.37 us (4%)
  between operations  4.08 us (3%)
    all_gather x1, blocking collectives, per_device(): lax.all_gather(jnp.concatenate([mine_h, slab], axis=0), 'zh', axis=0)  38.7 us
    ppermute x1, waiting for transfers between devices, per_device(): return lax.ppermute(k_block.reshape(-1, LANES), ALL, swapped_pairs())  15.4 us
    all_to_all x1, starting transfers between devices, per_device(): got = lax.all_to_all(packed, PLANE, 0, 0, tiled=True)  7.17 us
    ppermute x2, starting transfers between devices, per_device(): lax.ppermute(own, 'x', [(x, (x + back) % 4) for x in range(4)])  6.96 us
    all_to_all x1, starting transfers between devices, per_device(): y_col = lax.all_to_all(copies, ROW, 0, 0, tiled=True)  6.62 us
    ppermute x1, starting transfers between devices, per_device(): slab = lax.ppermute(slab, ALL, swapped_pairs())  6.26 us
    ppermute x2, waiting for transfers between devices, per_device(): lax.ppermute(own, 'x', [(x, (x + back) % 4) for x in range(4)])  6.14 us
    all_to_all x1, starting transfers between devices, per_device(): all_z = lax.all_to_all(part_z, 'zl', 0, 0, tiled=True)  5.55 us
  transfers between devices with their start and end apart: 10, of which 6 were waited for; matrix products, arithmetic and copies ran while one was open for 1% of the time, Pallas kernels for 0%

profile of v4, /device:TPU:64, one launch (start us, length us, event | category | flops | bytes accessed | tf_op | source)
XLA Modules:
  0.0 143.7 jit_solution(17877664777848394866)
XLA Ops:
  0.0 2.6 %pick.1 = (bf16[16,3,64,128]{3,2,1,0:T(8,128)(2,1)}, bf16[2,64,128]{2,1,0:T(8,128)(2,1)}) custom-call(s32[2,16]{1,0:T(2,128)} %blocks.3, s32[2,32]{1,0:T(2,128)} %mask_h.1, s32[2,64]{1,0:T(2,128)} %bitcast.47, s32[2,2]{1,0:T(2,128)} %mask_slab.1, bf16[128,2048]{1,0:T(8,128)(2,1)} %h.1, bf16[4096,128]{1,0:T(8,128)(2,1)} %z.1, bf16[128,128]{1,0:T(8,128)(2,1)} %slab.1), custom_call_target="tpu_custom_call" | custom-call | tf_op jit(solution)/shard_map/pick/pallas_call | solution.py:104
  2.6 0.0 copy-start.8
  2.6 7.2 %all-to-all-start = ((bf16[16,3,64,128]{3,2,1,0:T(8,128)(2,1)}), bf16[16,3,64,128]{3,2,1,0:T(8,128)(2,1)S(1)}, u32[]{:S(2)}, u32[]{:S(2)}) async-start(bf16[16,3,64,128]{3,2,1,0:T(8,128)(2,1)} %get-tuple-element.21), calls=%async_computation | async-start | bytes 1572864 | tf_op jit(solution)/shard_map/all_to_all | solution.py:113
  9.8 0.0 copy-done.8
  9.8 6.3 %collective-permute-start = (bf16[2,64,128]{2,1,0:T(8,128)(2,1)S(1)}, bf16[2,64,128]{2,1,0:T(8,128)(2,1)S(1)}, u32[]{:S(2)}, u32[]{:S(2)}) collective-permute-start(bf16[2,64,128]{2,1,0:T(8,128)(2,1)S(1)} %copy-done.8), channel_id=1, source_target_pairs={{0,0},{1,1},{2,32},{3,33},{4,64},{5,65},{6,96},{7,97},{8,128},{9,1... | collective-permute-start | bytes 98312 | tf_op jit(solution)/shard_map/ppermute | solution.py:112
  16.1 0.0 copy-start.7
  16.1 0.7 copy-done.7
  16.8 0.5 fusion.4
  21.2 3.1 %all-to-all-done = bf16[16,3,64,128]{3,2,1,0:T(8,128)(2,1)S(1)} async-done(((bf16[16,3,64,128]{3,2,1,0:T(8,128)(2,1)}), bf16[16,3,64,128]{3,2,1,0:T(8,128)(2,1)S(1)}, u32[]{:S(2)}, u32[]{:S(2)}) %all-to-all-start) | async-done | bytes 786464 | tf_op jit(solution)/shard_map/all_to_all | solution.py:113
  24.3 0.1 fusion.3
  24.5 0.0 collective-permute-done
  24.5 0.9 broadcast_in_dim.6
  25.4 5.5 %all-to-all-start.1 = ((bf16[4,2,4,64,128]{4,3,2,1,0:T(8,128)(2,1)}), bf16[4,2,4,64,128]{4,3,2,1,0:T(8,128)(2,1)S(1)}, u32[]{:S(2)}, u32[]{:S(2)}) async-start(bf16[4,2,4,64,128]{4,3,2,1,0:T(8,128)(2,1)} %broadcast_in_dim.6), calls=%async_computation.1 | async-start | bytes 1048576 | tf_op jit(solution)/shard_map/all_to_all | solution.py:137
  31.0 2.0 %all-gather = bf16[4,4,64,128]{3,2,1,0:T(8,128)(2,1)S(1)} all-gather(bf16[2,4,64,128]{3,2,1,0:T(8,128)(2,1)S(1)} %pad_maximum_fusion.1), channel_id=2, replica_groups=mesh['zl'=4,'y'=4,'x'=4,'zh'=4,'co'=2] {'co'}, dimensions={0}, use_global_device_ids=true | all-gather | bytes 393216 | tf_op jit(solution)/shard_map/all_gather | solution.py:139
  33.0 38.7 %all-gather.1 = bf16[24,64,128]{2,1,0:T(8,128)(2,1)S(1)} all-gather(bf16[6,64,128]{2,1,0:T(8,128)(2,1)S(1)} %pad_maximum_fusion.3), channel_id=3, replica_groups=mesh['zl'=4,'y'=4,'x'=4,'zh'=4,'co'=2] {'zh'}, dimensions={0}, use_global_device_ids=true | all-gather | bytes 491520 | tf_op jit(solution)/shard_map/all_gather | solution.py:142
  71.7 2.5 %all-gather.2 = bf16[8,6,64,128]{3,2,1,0:T(8,128)(2,1)} all-gather(bf16[4,6,64,128]{3,2,1,0:T(8,128)(2,1)S(1)} %bitcast.37), channel_id=4, replica_groups=mesh['zl'=4,'y'=4,'x'=4,'zh'=4,'co'=2] {'co'}, dimensions={0}, use_global_device_ids=true | all-gather | bytes 1179648 | tf_op jit(solution)/shard_map/all_gather | solution.py:143
  74.2 0.0 all-to-all-done.1.all_z
  74.2 0.0 copy-start
  74.2 0.8 copy-done
  75.0 2.5 %product.1 = bf16[16,128,128]{2,1,0:T(8,128)(2,1)} custom-call(s32[2,16]{1,0:T(2,128)} %blocks.3, bf16[2,4,6,64,128]{4,3,2,1,0:T(8,128)(2,1)} %bitcast.34, bf16[4,2,4,64,128]{4,3,2,1,0:T(8,128)(2,1)} %copy-done), custom_call_target="tpu_custom_call" | custom-call | tf_op jit(solution)/shard_map/product/pallas_call | solution.py:144
  77.4 4.8 %all-to-all-start.2 = ((bf16[16,128,128]{2,1,0:T(8,128)(2,1)}), bf16[16,128,128]{2,1,0:T(8,128)(2,1)S(1)}, u32[]{:S(2)}, u32[]{:S(2)}) async-start(bf16[16,128,128]{2,1,0:T(8,128)(2,1)} %product.1), calls=%async_computation.2 | async-start | bytes 1048576 | tf_op jit(solution)/shard_map/all_to_all | solution.py:151
  82.2 5.0 %collective-permute-start.2 = (bf16[4,128,128]{2,1,0:T(8,128)(2,1)S(1)}, bf16[4,128,128]{2,1,0:T(8,128)(2,1)S(1)}, u32[]{:S(2)}, u32[]{:S(2)}) collective-permute-start(bf16[4,128,128]{2,1,0:T(8,128)(2,1)S(1)} %bitcast.44), channel_id=1, source_target_pairs={{0,24},{8,0},{16,8},{24,16},{1,25},{9,1},{17,9},{25,17},{2,26},{10... | collective-permute-start | bytes 393224 | tf_op jit(solution)/shard_map/ppermute | solution.py:155
  87.3 1.9 %collective-permute-start.1 = (bf16[4,128,128]{2,1,0:T(8,128)(2,1)S(1)}, bf16[4,128,128]{2,1,0:T(8,128)(2,1)S(1)}, u32[]{:S(2)}, u32[]{:S(2)}) collective-permute-start(bf16[4,128,128]{2,1,0:T(8,128)(2,1)S(1)} %bitcast.45), channel_id=1, source_target_pairs={{0,8},{8,16},{16,24},{24,0},{1,9},{9,17},{17,25},{25,1},{2,10},{10... | collective-permute-start | bytes 393224 | tf_op jit(solution)/shard_map/ppermute | solution.py:155
  89.2 4.0 %collective-permute-done.2.three = bf16[4,128,128]{2,1,0:T(8,128)(2,1)S(1)} collective-permute-done((bf16[4,128,128]{2,1,0:T(8,128)(2,1)S(1)}, bf16[4,128,128]{2,1,0:T(8,128)(2,1)S(1)}, u32[]{:S(2)}, u32[]{:S(2)}) %collective-permute-start.2) | collective-permute-done | bytes 131104 | tf_op jit(solution)/shard_map/ppermute | solution.py:155
  93.2 0.0 copy-start.3
  93.2 2.1 %collective-permute-done.1.one = bf16[4,128,128]{2,1,0:T(8,128)(2,1)S(1)} collective-permute-done((bf16[4,128,128]{2,1,0:T(8,128)(2,1)S(1)}, bf16[4,128,128]{2,1,0:T(8,128)(2,1)S(1)}, u32[]{:S(2)}, u32[]{:S(2)}) %collective-permute-start.1) | collective-permute-done | bytes 131104 | tf_op jit(solution)/shard_map/ppermute | solution.py:155
  95.4 0.0 all-to-all-done.2
  95.4 0.1 reduce_sum.12
  95.4 0.9 broadcast_in_dim.7
  96.4 6.6 %all-to-all-start.3 = ((bf16[16,128,128]{2,1,0:T(8,128)(2,1)}), bf16[16,128,128]{2,1,0:T(8,128)(2,1)S(1)}, u32[]{:S(2)}, u32[]{:S(2)}) async-start(bf16[16,128,128]{2,1,0:T(8,128)(2,1)} %broadcast_in_dim.7), calls=%async_computation.3 | async-start | bytes 1048576 | tf_op jit(solution)/shard_map/all_to_all | solution.py:162
  103.0 1.0 slice.43
  104.0 0.0 copy-start.2
  104.0 2.5 %collective-permute-start.3 = (bf16[2,4,128,128]{3,2,1,0:T(8,128)(2,1)S(1)}, bf16[2,4,128,128]{3,2,1,0:T(8,128)(2,1)S(1)}, u32[]{:S(2)}, u32[]{:S(2)}) collective-permute-start(bf16[2,4,128,128]{3,2,1,0:T(8,128)(2,1)S(1)} %bitcast.39), channel_id=1, source_target_pairs={{0,16},{8,24},{16,0},{24,8},{1,17},{9,25},{17,1},{25,9},{2,18},{10... | collective-permute-start | bytes 786440 | tf_op jit(solution)/shard_map/ppermute | solution.py:157
  106.5 0.0 copy-done.3
  106.5 0.0 copy-done.4
  106.5 0.0 copy-done.2
  106.5 1.9 %collective-permute-start.4 = (bf16[2,4,128,128]{3,2,1,0:T(8,128)(2,1)S(1)}, bf16[2,4,128,128]{3,2,1,0:T(8,128)(2,1)S(1)}, u32[]{:S(2)}, u32[]{:S(2)}) collective-permute-start(bf16[2,4,128,128]{3,2,1,0:T(8,128)(2,1)S(1)} %pad_maximum_fusion), channel_id=1, source_target_pairs={{0,1},{1,0},{2,3},{3,2},{4,5},{5,4},{6,7},{7,6},{8,9},{9,8},{10,11... | collective-permute-start | bytes 786440 | tf_op jit(solution)/shard_map/ppermute | solution.py:159
  108.5 5.3 %collective-permute-done.3.two = bf16[2,4,128,128]{3,2,1,0:T(8,128)(2,1)S(1)} collective-permute-done((bf16[2,4,128,128]{3,2,1,0:T(8,128)(2,1)S(1)}, bf16[2,4,128,128]{3,2,1,0:T(8,128)(2,1)S(1)}, u32[]{:S(2)}, u32[]{:S(2)}) %collective-permute-start.3) | collective-permute-done | bytes 262176 | tf_op jit(solution)/shard_map/ppermute | solution.py:157
  113.7 0.0 collective-permute-done.4.swapped
  113.8 2.2 %all-to-all-done.3.y_col = bf16[16,128,128]{2,1,0:T(8,128)(2,1)S(1)} async-done(((bf16[16,128,128]{2,1,0:T(8,128)(2,1)}), bf16[16,128,128]{2,1,0:T(8,128)(2,1)S(1)}, u32[]{:S(2)}, u32[]{:S(2)}) %all-to-all-start.3) | async-done | bytes 524320 | tf_op jit(solution)/shard_map/all_to_all | solution.py:162
  116.0 0.0 copy-done.5
  116.0 0.0 copy-done.6
  116.0 0.8 copy-done.1
  116.8 2.5 %last.1 = bf16[2,128,128]{2,1,0:T(8,128)(2,1)} custom-call(bf16[16,128,128]{2,1,0:T(8,128)(2,1)} %copy-done.1, bf16[2,4,128,128]{3,2,1,0:T(8,128)(2,1)} %bitcast.40, bf16[2,4,128,128]{3,2,1,0:T(8,128)(2,1)} %copy-done.5, bf16[4,128,128]{2,1,0:T(8,128)(2,1)} %copy-done.4, bf16[4,128,128]{2,1,0:T(8,128)(2,1)} %copy-done.3, bf16[2,4,128,128]{3,2,1,0:T(8,128)(2,1)} %copy-done.6), custom_call_target="tpu_custom_call" | custom-call | tf_op jit(solution)/shard_map/last/pallas_call | solution.py:163
  119.2 4.7 %all_to_all.25 = bf16[2,128,128]{2,1,0:T(8,128)(2,1)S(1)} all-to-all(bf16[2,128,128]{2,1,0:T(8,128)(2,1)} %last.1), channel_id=1, replica_groups=mesh['zl'=4,'y'=4,'x'=4,'zh'=4,'co'=2] {'co'}, dimensions={0} | all-to-all | bytes 131072 | tf_op jit(solution)/shard_map/all_to_all | solution.py:170
  123.9 3.8 %collective-permute-start.5 = (bf16[256,128]{1,0:T(8,128)(2,1)S(1)}, bf16[256,128]{1,0:T(8,128)(2,1)S(1)}, u32[]{:S(2)}, u32[]{:S(2)}) collective-permute-start(bf16[256,128]{1,0:T(8,128)(2,1)S(1)} %bitcast.46), channel_id=1, source_target_pairs={{0,0},{1,1},{2,32},{3,33},{4,64},{5,65},{6,96},{7,97},{8,128},{9,1... | collective-permute-start | bytes 196616 | tf_op jit(solution)/shard_map/ppermute | solution.py:171
  127.7 15.4 %collective-permute-done.5 = bf16[256,128]{1,0:T(8,128)(2,1)S(1)} collective-permute-done((bf16[256,128]{1,0:T(8,128)(2,1)S(1)}, bf16[256,128]{1,0:T(8,128)(2,1)S(1)}, u32[]{:S(2)}, u32[]{:S(2)}) %collective-permute-start.5) | collective-permute-done | bytes 65568 | tf_op jit(solution)/shard_map/ppermute | solution.py:171
  143.1 0.6 copy.14
  (12 shorter events, 0.1 us)
Async XLA Ops:
  2.6 7.2 %copy-start.8 = (bf16[2,64,128]{2,1,0:T(8,128)(2,1)S(1)}, bf16[2,64,128]{2,1,0:T(8,128)(2,1)}, u32[]{:S(2)}) copy-start(bf16[2,64,128]{2,1,0:T(8,128)(2,1)} %get-tuple-element.20) | copy-start | bytes 98308
  2.6 21.7 %all-to-all-start = ((bf16[16,3,64,128]{3,2,1,0:T(8,128)(2,1)}), bf16[16,3,64,128]{3,2,1,0:T(8,128)(2,1)S(1)}, u32[]{:S(2)}, u32[]{:S(2)}) async-start(bf16[16,3,64,128]{3,2,1,0:T(8,128)(2,1)} %get-tuple-element.21), calls=%async_computation | async-start | bytes 1572864 | tf_op jit(solution)/shard_map/all_to_all | solution.py:113
  9.8 14.7 %collective-permute-start = (bf16[2,64,128]{2,1,0:T(8,128)(2,1)S(1)}, bf16[2,64,128]{2,1,0:T(8,128)(2,1)S(1)}, u32[]{:S(2)}, u32[]{:S(2)}) collective-permute-start(bf16[2,64,128]{2,1,0:T(8,128)(2,1)S(1)} %copy-done.8), channel_id=1, source_target_pairs={{0,0},{1,1},{2,32},{3,33},{4,64},{5,65},{6,96},{7,97},{8,128},{9,1... | collective-permute-start | bytes 98312 | tf_op jit(solution)/shard_map/ppermute | solution.py:112
  16.1 0.7 copy-start.7
  25.4 48.7 %all-to-all-start.1 = ((bf16[4,2,4,64,128]{4,3,2,1,0:T(8,128)(2,1)}), bf16[4,2,4,64,128]{4,3,2,1,0:T(8,128)(2,1)S(1)}, u32[]{:S(2)}, u32[]{:S(2)}) async-start(bf16[4,2,4,64,128]{4,3,2,1,0:T(8,128)(2,1)} %broadcast_in_dim.6), calls=%async_computation.1 | async-start | bytes 1048576 | tf_op jit(solution)/shard_map/all_to_all | solution.py:137
  74.2 0.8 copy-start
  77.4 17.9 %all-to-all-start.2 = ((bf16[16,128,128]{2,1,0:T(8,128)(2,1)}), bf16[16,128,128]{2,1,0:T(8,128)(2,1)S(1)}, u32[]{:S(2)}, u32[]{:S(2)}) async-start(bf16[16,128,128]{2,1,0:T(8,128)(2,1)} %product.1), calls=%async_computation.2 | async-start | bytes 1048576 | tf_op jit(solution)/shard_map/all_to_all | solution.py:151
  82.2 11.0 %collective-permute-start.2 = (bf16[4,128,128]{2,1,0:T(8,128)(2,1)S(1)}, bf16[4,128,128]{2,1,0:T(8,128)(2,1)S(1)}, u32[]{:S(2)}, u32[]{:S(2)}) collective-permute-start(bf16[4,128,128]{2,1,0:T(8,128)(2,1)S(1)} %bitcast.44), channel_id=1, source_target_pairs={{0,24},{8,0},{16,8},{24,16},{1,25},{9,1},{17,9},{25,17},{2,26},{10... | collective-permute-start | bytes 393224 | tf_op jit(solution)/shard_map/ppermute | solution.py:155
  87.3 8.1 %collective-permute-start.1 = (bf16[4,128,128]{2,1,0:T(8,128)(2,1)S(1)}, bf16[4,128,128]{2,1,0:T(8,128)(2,1)S(1)}, u32[]{:S(2)}, u32[]{:S(2)}) collective-permute-start(bf16[4,128,128]{2,1,0:T(8,128)(2,1)S(1)} %bitcast.45), channel_id=1, source_target_pairs={{0,8},{8,16},{16,24},{24,0},{1,9},{9,17},{17,25},{25,1},{2,10},{10... | collective-permute-start | bytes 393224 | tf_op jit(solution)/shard_map/ppermute | solution.py:155
  93.2 13.2 %copy-start.3 = (bf16[4,128,128]{2,1,0:T(8,128)(2,1)}, bf16[4,128,128]{2,1,0:T(8,128)(2,1)S(1)}, u32[]{:S(2)}) copy-start(bf16[4,128,128]{2,1,0:T(8,128)(2,1)S(1)} %collective-permute-done.2.three) | copy-start | bytes 393220
  95.4 11.1 %copy-start.4 = (bf16[4,128,128]{2,1,0:T(8,128)(2,1)}, bf16[4,128,128]{2,1,0:T(8,128)(2,1)S(1)}, u32[]{:S(2)}) copy-start(bf16[4,128,128]{2,1,0:T(8,128)(2,1)S(1)} %collective-permute-done.1.one) | copy-start | bytes 393220
  96.4 19.6 %all-to-all-start.3 = ((bf16[16,128,128]{2,1,0:T(8,128)(2,1)}), bf16[16,128,128]{2,1,0:T(8,128)(2,1)S(1)}, u32[]{:S(2)}, u32[]{:S(2)}) async-start(bf16[16,128,128]{2,1,0:T(8,128)(2,1)} %broadcast_in_dim.7), calls=%async_computation.3 | async-start | bytes 1048576 | tf_op jit(solution)/shard_map/all_to_all | solution.py:162
  104.0 2.6 %copy-start.2 = (bf16[2,4,2,64,128]{4,3,2,1,0:T(8,128)(2,1)}, bf16[2,4,2,64,128]{4,3,2,1,0:T(8,128)(2,1)S(1)}, u32[]{:S(2)}) copy-start(bf16[2,4,2,64,128]{4,3,2,1,0:T(8,128)(2,1)S(1)} %slice.43) | copy-start | bytes 786436
  104.0 9.8 %collective-permute-start.3 = (bf16[2,4,128,128]{3,2,1,0:T(8,128)(2,1)S(1)}, bf16[2,4,128,128]{3,2,1,0:T(8,128)(2,1)S(1)}, u32[]{:S(2)}, u32[]{:S(2)}) collective-permute-start(bf16[2,4,128,128]{3,2,1,0:T(8,128)(2,1)S(1)} %bitcast.39), channel_id=1, source_target_pairs={{0,16},{8,24},{16,0},{24,8},{1,17},{9,25},{17,1},{25,9},{2,18},{10... | collective-permute-start | bytes 786440 | tf_op jit(solution)/shard_map/ppermute | solution.py:157
  106.5 7.2 %collective-permute-start.4 = (bf16[2,4,128,128]{3,2,1,0:T(8,128)(2,1)S(1)}, bf16[2,4,128,128]{3,2,1,0:T(8,128)(2,1)S(1)}, u32[]{:S(2)}, u32[]{:S(2)}) collective-permute-start(bf16[2,4,128,128]{3,2,1,0:T(8,128)(2,1)S(1)} %pad_maximum_fusion), channel_id=1, source_target_pairs={{0,1},{1,0},{2,3},{3,2},{4,5},{5,4},{6,7},{7,6},{8,9},{9,8},{10,11... | collective-permute-start | bytes 786440 | tf_op jit(solution)/shard_map/ppermute | solution.py:159
  113.7 2.2 %copy-start.5 = (bf16[2,4,128,128]{3,2,1,0:T(8,128)(2,1)}, bf16[2,4,128,128]{3,2,1,0:T(8,128)(2,1)S(1)}, u32[]{:S(2)}) copy-start(bf16[2,4,128,128]{3,2,1,0:T(8,128)(2,1)S(1)} %collective-permute-done.3.two) | copy-start | bytes 786436
  113.7 2.2 %copy-start.6 = (bf16[2,4,128,128]{3,2,1,0:T(8,128)(2,1)}, bf16[2,4,128,128]{3,2,1,0:T(8,128)(2,1)S(1)}, u32[]{:S(2)}) copy-start(bf16[2,4,128,128]{3,2,1,0:T(8,128)(2,1)S(1)} %collective-permute-done.4.swapped) | copy-start | bytes 786436
  116.0 0.8 copy-start.1
  123.9 19.2 %collective-permute-start.5 = (bf16[256,128]{1,0:T(8,128)(2,1)S(1)}, bf16[256,128]{1,0:T(8,128)(2,1)S(1)}, u32[]{:S(2)}, u32[]{:S(2)}) collective-permute-start(bf16[256,128]{1,0:T(8,128)(2,1)S(1)} %bitcast.46), channel_id=1, source_target_pairs={{0,0},{1,1},{2,32},{3,33},{4,64},{5,65},{6,96},{7,97},{8,128},{9,1... | collective-permute-start | bytes 196616 | tf_op jit(solution)/shard_map/ppermute | solution.py:171

commit v5 on v4

--- a/solution.py
+++ b/solution.py
@@ -1,3 +1,5 @@
+import functools
+
 import jax
 import jax.numpy as jnp
 from jax import lax
@@ -55,11 +57,12 @@
         masked[i] = slab[at, :] * lane_mask(mask_slab[i, 0], mask_slab[i, 1])
 
 
-def product_kernel(blocks, pair, all_z, out):
+def product_kernel(single, blocks, pair, all_z, out):
     z0 = [owner_row(blocks, s) // 4 for s in range(SECTIONS)]
     zh0 = [lax.rem(owner_col(blocks, s) // 2, 4) for s in range(SECTIONS)]
     right = [
-        jnp.concatenate([all_z[z0[s], s, x] for s in range(SECTIONS)], axis=0) for x in range(4)
+        jnp.concatenate([all_z[z0[s], 0 if single else s, x] for s in range(SECTIONS)], axis=0)
+        for x in range(4)
     ]
     for y in range(4):
         left = jnp.concatenate([pair[s, zh0[s], y] for s in range(SECTIONS)], axis=0)
@@ -132,22 +135,33 @@
             for s in range(SECTIONS)
         ]
     )
-    part_z = jnp.broadcast_to(part_z, (4,) + part_z.shape)
     slab, part_h, part_z = lax.optimization_barrier((slab, part_h, part_z))
-    all_z = lax.all_to_all(part_z, "zl", 0, 0, tiled=True)
     core = lax.axis_index("co")
-    pair_h = lax.all_gather(part_h, "co", axis=0)
-    mine_h = lax.dynamic_index_in_dim(pair_h, core, 1, keepdims=False)
-    mine_h = mine_h[0] + mine_h[1]
-    across = lax.all_gather(jnp.concatenate([mine_h, slab], axis=0), "zh", axis=0)
-    pair = lax.all_gather(across, "co", axis=0)
-    partial = pl.pallas_call(
-        product_kernel,
-        out_shape=shape(16, LANES, LANES),
-        in_specs=[SMEM, VMEM, VMEM],
-        out_specs=VMEM,
-        name="product",
-    )(blocks, pair, all_z)
+
+    def partial_product(part_z, single):
+        all_z = lax.all_to_all(
+            jnp.broadcast_to(part_z, (4,) + part_z.shape), "zl", 0, 0, tiled=True
+        )
+        pair_h = lax.all_gather(part_h, "co", axis=0)
+        mine_h = lax.dynamic_index_in_dim(pair_h, core, 1, keepdims=False)
+        mine_h = mine_h[0] + mine_h[1]
+        across = lax.all_gather(jnp.concatenate([mine_h, slab], axis=0), "zh", axis=0)
+        pair = lax.all_gather(across, "co", axis=0)
+        partial = pl.pallas_call(
+            functools.partial(product_kernel, single),
+            out_shape=shape(16, LANES, LANES),
+            in_specs=[SMEM, VMEM, VMEM],
+            out_specs=VMEM,
+            name="product",
+        )(blocks, pair, all_z)
+        return partial, across, pair
+
+    own_section = jnp.where(outer[1] == lax.axis_index("zl"), 1, 0)
+    partial, across, pair = lax.cond(
+        outer[0] == outer[1],
+        lambda: partial_product(part_z, False),
+        lambda: partial_product(lax.dynamic_slice_in_dim(part_z, own_section, 1, 0), True),
+    )
     partial = lax.all_to_all(partial, PLANE, 0, 0, tiled=True)
     own = across[:, 4:].reshape(4, LANES, LANES)
     both = pair[:, :, 4:].reshape(2, 4, LANES, LANES)

time: 145 us -> 145 us (level)
  blocking collectives: 47.9 us -> 39.7 us
  starting transfers between devices: 45.5 us -> 50.6 us
  waiting for transfers between devices: 32.2 us -> 34.9 us
    all_gather x3, blocking collectives: 43.2 us -> 35 us  [the longest x1 30.6 us: partial_product(): lax.all_gather(jnp.concatenate([mine_h, slab], axis=0), 'zh', axis=0)]
    all_to_all x1, starting transfers between devices: 4.78 us -> 7.37 us  [per_device(): partial = lax.all_to_all(partial, PLANE, 0, 0, tiled=True)]
    cond x0 -> x6, local copies, waits for them, and re-layouts: none -> 2.57 us
    all_to_all x1, starting transfers between devices: 6.62 us -> 8.33 us  [per_device(): y_col = lax.all_to_all(copies, ROW, 0, 0, tiled=True)]
    unnamed x19 -> x17, local copies, waits for them, and re-layouts: 2.92 us -> 2.12 us
where the time goes in v5:
time: 145 us; the launch traced here: 144 us
  starting transfers between devices  50.6 us (35%)
  blocking collectives  39.7 us (27%)
  waiting for transfers between devices  34.9 us (24%)
  Pallas kernels  7.51 us (5%)
  local copies, waits for them, and re-layouts  7 us (5%)
  between operations  3.89 us (3%)
    all_gather x1, blocking collectives, partial_product(): lax.all_gather(jnp.concatenate([mine_h, slab], axis=0), 'zh', axis=0)  30.6 us
    ppermute x1, waiting for transfers between devices, per_device(): return lax.ppermute(k_block.reshape(-1, LANES), ALL, swapped_pairs())  16.1 us
    all_to_all x1, starting transfers between devices, per_device(): y_col = lax.all_to_all(copies, ROW, 0, 0, tiled=True)  8.33 us
    all_to_all x1, starting transfers between devices, per_device(): partial = lax.all_to_all(partial, PLANE, 0, 0, tiled=True)  7.37 us
    all_to_all x1, starting transfers between devices, per_device(): got = lax.all_to_all(packed, PLANE, 0, 0, tiled=True)  7.17 us
    ppermute x2, starting transfers between devices, per_device(): lax.ppermute(own, 'x', [(x, (x + back) % 4) for x in range(4)])  7.05 us
    ppermute x1, starting transfers between devices, per_device(): slab = lax.ppermute(slab, ALL, swapped_pairs())  6.26 us
    all_to_all x1, starting transfers between devices, partial_product(): lax.all_to_all(jnp.broadcast_to(part_z, (4,) + part_z.shape), 'zl', 0, 0,...  5.55 us
  transfers between devices with their start and end apart: 10, of which 6 were waited for; matrix products, arithmetic and copies ran while one was open for 1% of the time, Pallas kernels for 0%

profile of v5, /device:TPU:64, one launch (start us, length us, event | category | flops | bytes accessed | tf_op | source)
XLA Modules:
  0.0 143.8 jit_solution(10245097356534893969)
XLA Ops:
  0.0 0.7 copy-done.10
  0.7 2.7 %pick.1 = (bf16[16,3,64,128]{3,2,1,0:T(8,128)(2,1)}, bf16[2,64,128]{2,1,0:T(8,128)(2,1)}) custom-call(s32[2,16]{1,0:T(2,128)S(1)} %copy-done.10, s32[2,32]{1,0:T(2,128)} %mask_h.1, s32[2,64]{1,0:T(2,128)} %bitcast.57, s32[2,2]{1,0:T(2,128)} %mask_slab.1, bf16[128,2048]{1,0:T(8,128)(2,1)} %h.1, bf16[4096,128]{1,0:T(8,128)(2,1)} %z.1, bf16[128,128]{1,0:T(8,128)(2,1)} %slab.1), custom_call_target="tpu_custom_call" | custom-call | tf_op jit(solution)/shard_map/pick/pallas_call | solution.py:107
  3.3 0.0 copy-start.11
  3.3 7.2 %all-to-all-start.2 = ((bf16[16,3,64,128]{3,2,1,0:T(8,128)(2,1)}), bf16[16,3,64,128]{3,2,1,0:T(8,128)(2,1)S(1)}, u32[]{:S(2)}, u32[]{:S(2)}) async-start(bf16[16,3,64,128]{3,2,1,0:T(8,128)(2,1)} %get-tuple-element.77), calls=%async_computation.2 | async-start | bytes 1572864 | tf_op jit(solution)/shard_map/all_to_all | solution.py:116
  10.5 0.0 copy-done.11
  10.5 6.3 %collective-permute-start = (bf16[2,64,128]{2,1,0:T(8,128)(2,1)S(1)}, bf16[2,64,128]{2,1,0:T(8,128)(2,1)S(1)}, u32[]{:S(2)}, u32[]{:S(2)}) collective-permute-start(bf16[2,64,128]{2,1,0:T(8,128)(2,1)S(1)} %copy-done.11), channel_id=1, source_target_pairs={{0,0},{1,1},{2,32},{3,33},{4,64},{5,65},{6,96},{7,97},{8,128},{9,1... | collective-permute-start | bytes 98312 | tf_op jit(solution)/shard_map/ppermute | solution.py:115
  16.8 0.5 fusion.5
  21.0 4.0 %all-to-all-done.2 = bf16[16,3,64,128]{3,2,1,0:T(8,128)(2,1)S(1)} async-done(((bf16[16,3,64,128]{3,2,1,0:T(8,128)(2,1)}), bf16[16,3,64,128]{3,2,1,0:T(8,128)(2,1)S(1)}, u32[]{:S(2)}, u32[]{:S(2)}) %all-to-all-start.2) | async-done | bytes 786464 | tf_op jit(solution)/shard_map/all_to_all | solution.py:116
  25.0 0.1 fusion.4
  25.2 0.0 collective-permute-done
  25.2 46.4 %conditional.1 = (bf16[16,128,128]{2,1,0:T(8,128)(2,1)}, bf16[4,6,64,128]{3,2,1,0:T(8,128)(2,1)}, bf16[4,6,64,128]{3,2,1,0:T(8,128)(2,1)S(1)}, bf16[2,4,6,64,128...) conditional(s32[]{:T(128)} %convert_element_type.13, (bf16[2,4,64,128]{3,2,1,0:T(8,128)(2,1)S(1)}, s32[]{:T(128)}, ...), branch_computations={%region_0.1_spmd, %region_1.2_spmd} | conditional | flops 81926 | bytes 10715318 | solution.py:160
  25.2 0.8 broadcast_in_dim.6
  26.0 5.5 %all-to-all-start = ((bf16[4,1,4,64,128]{4,3,2,1,0:T(8,128)(2,1)}), bf16[4,1,4,64,128]{4,3,2,1,0:T(8,128)(2,1)S(1)}, u32[]{:S(2)}, u32[]{:S(2)}) async-start(bf16[4,1,4,64,128]{4,3,2,1,0:T(8,128)(2,1)} %broadcast_in_dim.6), calls=%async_computation | async-start | bytes 524288 | tf_op jit(solution)/shard_map/cond/branch_0_fun/all_to_all | solution.py:142
  31.6 2.0 %all-gather = bf16[4,4,64,128]{3,2,1,0:T(8,128)(2,1)S(1)} all-gather(bf16[2,4,64,128]{3,2,1,0:T(8,128)(2,1)S(1)} %get-tuple-element.48), channel_id=2, replica_groups=mesh['zl'=4,'y'=4,'x'=4,'zh'=4,'co'=2] {'co'}, dimensions={0}, use_global_device_ids=true | all-gather | bytes 393216 | tf_op jit(solution)/shard_map/cond/branch_0_fun/all_gather | solution.py:145
  33.6 30.6 %all-gather.1 = bf16[24,64,128]{2,1,0:T(8,128)(2,1)S(1)} all-gather(bf16[6,64,128]{2,1,0:T(8,128)(2,1)S(1)} %pad_maximum_fusion), channel_id=3, replica_groups=mesh['zl'=4,'y'=4,'x'=4,'zh'=4,'co'=2] {'zh'}, dimensions={0}, use_global_device_ids=true | all-gather | bytes 491520 | tf_op jit(solution)/shard_map/cond/branch_0_fun/all_gather | solution.py:148
  64.1 0.0 copy-start
  64.2 0.7 copy-done
  64.9 2.5 %all-gather.2 = bf16[8,6,64,128]{3,2,1,0:T(8,128)(2,1)} all-gather(bf16[4,6,64,128]{3,2,1,0:T(8,128)(2,1)S(1)} %bitcast.42), channel_id=4, replica_groups=mesh['zl'=4,'y'=4,'x'=4,'zh'=4,'co'=2] {'co'}, dimensions={0}, use_global_device_ids=true | all-gather | bytes 1179648 | tf_op jit(solution)/shard_map/cond/branch_0_fun/all_gather | solution.py:149
  67.4 1.1 copy.24
  68.5 0.0 all-to-all-done.all_z
  68.5 0.7 copy-done.5
  69.2 2.4 %product.2 = bf16[16,128,128]{2,1,0:T(8,128)(2,1)} custom-call(s32[2,16]{1,0:T(2,128)S(1)} %get-tuple-element.47.blocks, bf16[2,4,6,64,128]{4,3,2,1,0:T(8,128)(2,1)} %bitcast.3.pair, bf16[4,1,4,64,128]{4,3,2,1,0:T(8,128)(2,1)} %copy-done.5), custom_call_target="tpu_custom_call" | custom-call | tf_op jit(solution)/shard_map/cond/branch_0_fun/product/pallas_call | solution.py:150
  71.6 7.4 %all-to-all-start.3 = ((bf16[16,128,128]{2,1,0:T(8,128)(2,1)}), bf16[16,128,128]{2,1,0:T(8,128)(2,1)S(1)}, u32[]{:S(2)}, u32[]{:S(2)}) async-start(bf16[16,128,128]{2,1,0:T(8,128)(2,1)} %get-tuple-element.97), calls=%async_computation.3 | async-start | bytes 1048576 | tf_op jit(solution)/shard_map/all_to_all | solution.py:165
  79.0 3.8 %collective-permute-start.1 = (bf16[4,128,128]{2,1,0:T(8,128)(2,1)S(1)}, bf16[4,128,128]{2,1,0:T(8,128)(2,1)S(1)}, u32[]{:S(2)}, u32[]{:S(2)}) collective-permute-start(bf16[4,128,128]{2,1,0:T(8,128)(2,1)S(1)} %bitcast.54), channel_id=1, source_target_pairs={{0,8},{8,16},{16,24},{24,0},{1,9},{9,17},{17,25},{25,1},{2,10},{10... | collective-permute-start | bytes 393224 | tf_op jit(solution)/shard_map/ppermute | solution.py:169
  82.8 3.2 %collective-permute-start.2 = (bf16[4,128,128]{2,1,0:T(8,128)(2,1)S(1)}, bf16[4,128,128]{2,1,0:T(8,128)(2,1)S(1)}, u32[]{:S(2)}, u32[]{:S(2)}) collective-permute-start(bf16[4,128,128]{2,1,0:T(8,128)(2,1)S(1)} %bitcast.55), channel_id=1, source_target_pairs={{0,24},{8,0},{16,8},{24,16},{1,25},{9,1},{17,9},{25,17},{2,26},{10... | collective-permute-start | bytes 393224 | tf_op jit(solution)/shard_map/ppermute | solution.py:169
  86.0 5.1 %collective-permute-done.1.one = bf16[4,128,128]{2,1,0:T(8,128)(2,1)S(1)} collective-permute-done((bf16[4,128,128]{2,1,0:T(8,128)(2,1)S(1)}, bf16[4,128,128]{2,1,0:T(8,128)(2,1)S(1)}, u32[]{:S(2)}, u32[]{:S(2)}) %collective-permute-start.1) | collective-permute-done | bytes 131104 | tf_op jit(solution)/shard_map/ppermute | solution.py:169
  91.1 0.0 collective-permute-done.2.three
  91.2 0.7 all-to-all-done.3
  91.9 0.1 reduce_sum.12
  92.0 0.9 broadcast_in_dim.9
  92.8 8.3 %all-to-all-start.4 = ((bf16[16,128,128]{2,1,0:T(8,128)(2,1)}), bf16[16,128,128]{2,1,0:T(8,128)(2,1)S(1)}, u32[]{:S(2)}, u32[]{:S(2)}) async-start(bf16[16,128,128]{2,1,0:T(8,128)(2,1)} %broadcast_in_dim.9), calls=%async_computation.4 | async-start | bytes 1048576 | tf_op jit(solution)/shard_map/all_to_all | solution.py:176
  101.2 0.0 copy-start.4
  101.2 3.4 %collective-permute-start.3 = (bf16[2,4,128,128]{3,2,1,0:T(8,128)(2,1)S(1)}, bf16[2,4,128,128]{3,2,1,0:T(8,128)(2,1)S(1)}, u32[]{:S(2)}, u32[]{:S(2)}) collective-permute-start(bf16[2,4,128,128]{3,2,1,0:T(8,128)(2,1)S(1)} %bitcast.48), channel_id=1, source_target_pairs={{0,16},{8,24},{16,0},{24,8},{1,17},{9,25},{17,1},{25,9},{2,18},{10... | collective-permute-start | bytes 786440 | tf_op jit(solution)/shard_map/ppermute | solution.py:171
  104.6 0.0 copy-done.6
  104.6 0.0 copy-done.7
  104.7 0.0 copy-done.4
  104.7 1.9 %collective-permute-start.4 = (bf16[2,4,128,128]{3,2,1,0:T(8,128)(2,1)S(1)}, bf16[2,4,128,128]{3,2,1,0:T(8,128)(2,1)S(1)}, u32[]{:S(2)}, u32[]{:S(2)}) collective-permute-start(bf16[2,4,128,128]{3,2,1,0:T(8,128)(2,1)S(1)} %pad_maximum_fusion.2), channel_id=1, source_target_pairs={{0,1},{1,0},{2,3},{3,2},{4,5},{5,4},{6,7},{7,6},{8,9},{9,8},{10,11... | collective-permute-start | bytes 786440 | tf_op jit(solution)/shard_map/ppermute | solution.py:173
  106.6 5.4 %collective-permute-done.3.two = bf16[2,4,128,128]{3,2,1,0:T(8,128)(2,1)S(1)} collective-permute-done((bf16[2,4,128,128]{3,2,1,0:T(8,128)(2,1)S(1)}, bf16[2,4,128,128]{3,2,1,0:T(8,128)(2,1)S(1)}, u32[]{:S(2)}, u32[]{:S(2)}) %collective-permute-start.3) | collective-permute-done | bytes 262176 | tf_op jit(solution)/shard_map/ppermute | solution.py:171
  112.0 0.0 collective-permute-done.4.swapped
  112.0 3.6 %all-to-all-done.4.y_col = bf16[16,128,128]{2,1,0:T(8,128)(2,1)S(1)} async-done(((bf16[16,128,128]{2,1,0:T(8,128)(2,1)}), bf16[16,128,128]{2,1,0:T(8,128)(2,1)S(1)}, u32[]{:S(2)}, u32[]{:S(2)}) %all-to-all-start.4) | async-done | bytes 524320 | tf_op jit(solution)/shard_map/all_to_all | solution.py:176
  115.6 0.0 copy-done.8
  115.6 0.0 copy-done.9
  115.6 0.8 copy-done.3
  116.4 2.5 %last.1 = bf16[2,128,128]{2,1,0:T(8,128)(2,1)} custom-call(bf16[16,128,128]{2,1,0:T(8,128)(2,1)} %copy-done.3, bf16[2,4,128,128]{3,2,1,0:T(8,128)(2,1)} %bitcast.49, bf16[2,4,128,128]{3,2,1,0:T(8,128)(2,1)} %copy-done.8, bf16[4,128,128]{2,1,0:T(8,128)(2,1)} %copy-done.6, bf16[4,128,128]{2,1,0:T(8,128)(2,1)} %copy-done.7, bf16[2,4,128,128]{3,2,1,0:T(8,128)(2,1)} %copy-done.9), custom_call_target="tpu_custom_call" | custom-call | tf_op jit(solution)/shard_map/last/pallas_call | solution.py:177
  118.8 4.7 %all_to_all.28 = bf16[2,128,128]{2,1,0:T(8,128)(2,1)S(1)} all-to-all(bf16[2,128,128]{2,1,0:T(8,128)(2,1)} %last.1), channel_id=1, replica_groups=mesh['zl'=4,'y'=4,'x'=4,'zh'=4,'co'=2] {'co'}, dimensions={0} | all-to-all | bytes 131072 | tf_op jit(solution)/shard_map/all_to_all | solution.py:184
  123.5 3.5 %collective-permute-start.5 = (bf16[256,128]{1,0:T(8,128)(2,1)S(1)}, bf16[256,128]{1,0:T(8,128)(2,1)S(1)}, u32[]{:S(2)}, u32[]{:S(2)}) collective-permute-start(bf16[256,128]{1,0:T(8,128)(2,1)S(1)} %bitcast.56), channel_id=1, source_target_pairs={{0,0},{1,1},{2,32},{3,33},{4,64},{5,65},{6,96},{7,97},{8,128},{9,1... | collective-permute-start | bytes 196616 | tf_op jit(solution)/shard_map/ppermute | solution.py:185
  127.1 16.1 %collective-permute-done.5 = bf16[256,128]{1,0:T(8,128)(2,1)S(1)} collective-permute-done((bf16[256,128]{1,0:T(8,128)(2,1)S(1)}, bf16[256,128]{1,0:T(8,128)(2,1)S(1)}, u32[]{:S(2)}, u32[]{:S(2)}) %collective-permute-start.5) | collective-permute-done | bytes 65568 | tf_op jit(solution)/shard_map/ppermute | solution.py:185
  143.1 0.6 copy.28
  (18 shorter events, 0.2 us)
Async XLA Ops:
  0.0 0.7 copy-start.10
  3.3 7.2 %copy-start.11 = (bf16[2,64,128]{2,1,0:T(8,128)(2,1)S(1)}, bf16[2,64,128]{2,1,0:T(8,128)(2,1)}, u32[]{:S(2)}) copy-start(bf16[2,64,128]{2,1,0:T(8,128)(2,1)} %get-tuple-element.80) | copy-start | bytes 98308
  3.3 21.7 %all-to-all-start.2 = ((bf16[16,3,64,128]{3,2,1,0:T(8,128)(2,1)}), bf16[16,3,64,128]{3,2,1,0:T(8,128)(2,1)S(1)}, u32[]{:S(2)}, u32[]{:S(2)}) async-start(bf16[16,3,64,128]{3,2,1,0:T(8,128)(2,1)} %get-tuple-element.77), calls=%async_computation.2 | async-start | bytes 1572864 | tf_op jit(solution)/shard_map/all_to_all | solution.py:116
  10.5 14.7 %collective-permute-start = (bf16[2,64,128]{2,1,0:T(8,128)(2,1)S(1)}, bf16[2,64,128]{2,1,0:T(8,128)(2,1)S(1)}, u32[]{:S(2)}, u32[]{:S(2)}) collective-permute-start(bf16[2,64,128]{2,1,0:T(8,128)(2,1)S(1)} %copy-done.11), channel_id=1, source_target_pairs={{0,0},{1,1},{2,32},{3,33},{4,64},{5,65},{6,96},{7,97},{8,128},{9,1... | collective-permute-start | bytes 98312 | tf_op jit(solution)/shard_map/ppermute | solution.py:115
  26.0 42.5 %all-to-all-start = ((bf16[4,1,4,64,128]{4,3,2,1,0:T(8,128)(2,1)}), bf16[4,1,4,64,128]{4,3,2,1,0:T(8,128)(2,1)S(1)}, u32[]{:S(2)}, u32[]{:S(2)}) async-start(bf16[4,1,4,64,128]{4,3,2,1,0:T(8,128)(2,1)} %broadcast_in_dim.6), calls=%async_computation | async-start | bytes 524288 | tf_op jit(solution)/shard_map/cond/branch_0_fun/all_to_all | solution.py:142
  64.1 0.7 copy-start
  68.5 0.7 copy-start.5
  71.6 20.3 %all-to-all-start.3 = ((bf16[16,128,128]{2,1,0:T(8,128)(2,1)}), bf16[16,128,128]{2,1,0:T(8,128)(2,1)S(1)}, u32[]{:S(2)}, u32[]{:S(2)}) async-start(bf16[16,128,128]{2,1,0:T(8,128)(2,1)} %get-tuple-element.97), calls=%async_computation.3 | async-start | bytes 1048576 | tf_op jit(solution)/shard_map/all_to_all | solution.py:165
  79.0 12.2 %collective-permute-start.1 = (bf16[4,128,128]{2,1,0:T(8,128)(2,1)S(1)}, bf16[4,128,128]{2,1,0:T(8,128)(2,1)S(1)}, u32[]{:S(2)}, u32[]{:S(2)}) collective-permute-start(bf16[4,128,128]{2,1,0:T(8,128)(2,1)S(1)} %bitcast.54), channel_id=1, source_target_pairs={{0,8},{8,16},{16,24},{24,0},{1,9},{9,17},{17,25},{25,1},{2,10},{10... | collective-permute-start | bytes 393224 | tf_op jit(solution)/shard_map/ppermute | solution.py:169
  82.8 8.3 %collective-permute-start.2 = (bf16[4,128,128]{2,1,0:T(8,128)(2,1)S(1)}, bf16[4,128,128]{2,1,0:T(8,128)(2,1)S(1)}, u32[]{:S(2)}, u32[]{:S(2)}) collective-permute-start(bf16[4,128,128]{2,1,0:T(8,128)(2,1)S(1)} %bitcast.55), channel_id=1, source_target_pairs={{0,24},{8,0},{16,8},{24,16},{1,25},{9,1},{17,9},{25,17},{2,26},{10... | collective-permute-start | bytes 393224 | tf_op jit(solution)/shard_map/ppermute | solution.py:169
  91.1 13.5 %copy-start.6 = (bf16[4,128,128]{2,1,0:T(8,128)(2,1)}, bf16[4,128,128]{2,1,0:T(8,128)(2,1)S(1)}, u32[]{:S(2)}) copy-start(bf16[4,128,128]{2,1,0:T(8,128)(2,1)S(1)} %collective-permute-done.1.one) | copy-start | bytes 393220
  91.2 13.5 %copy-start.7 = (bf16[4,128,128]{2,1,0:T(8,128)(2,1)}, bf16[4,128,128]{2,1,0:T(8,128)(2,1)S(1)}, u32[]{:S(2)}) copy-start(bf16[4,128,128]{2,1,0:T(8,128)(2,1)S(1)} %collective-permute-done.2.three) | copy-start | bytes 393220
  92.8 22.7 %all-to-all-start.4 = ((bf16[16,128,128]{2,1,0:T(8,128)(2,1)}), bf16[16,128,128]{2,1,0:T(8,128)(2,1)S(1)}, u32[]{:S(2)}, u32[]{:S(2)}) async-start(bf16[16,128,128]{2,1,0:T(8,128)(2,1)} %broadcast_in_dim.9), calls=%async_computation.4 | async-start | bytes 1048576 | tf_op jit(solution)/shard_map/all_to_all | solution.py:176
  101.2 3.5 %copy-start.4 = (bf16[2,4,2,64,128]{4,3,2,1,0:T(8,128)(2,1)}, bf16[2,4,2,64,128]{4,3,2,1,0:T(8,128)(2,1)S(1)}, u32[]{:S(2)}) copy-start(bf16[2,4,2,64,128]{4,3,2,1,0:T(8,128)(2,1)S(1)} %slice.61) | copy-start | bytes 786436
  101.2 10.8 %collective-permute-start.3 = (bf16[2,4,128,128]{3,2,1,0:T(8,128)(2,1)S(1)}, bf16[2,4,128,128]{3,2,1,0:T(8,128)(2,1)S(1)}, u32[]{:S(2)}, u32[]{:S(2)}) collective-permute-start(bf16[2,4,128,128]{3,2,1,0:T(8,128)(2,1)S(1)} %bitcast.48), channel_id=1, source_target_pairs={{0,16},{8,24},{16,0},{24,8},{1,17},{9,25},{17,1},{25,9},{2,18},{10... | collective-permute-start | bytes 786440 | tf_op jit(solution)/shard_map/ppermute | solution.py:171
  104.7 7.3 %collective-permute-start.4 = (bf16[2,4,128,128]{3,2,1,0:T(8,128)(2,1)S(1)}, bf16[2,4,128,128]{3,2,1,0:T(8,128)(2,1)S(1)}, u32[]{:S(2)}, u32[]{:S(2)}) collective-permute-start(bf16[2,4,128,128]{3,2,1,0:T(8,128)(2,1)S(1)} %pad_maximum_fusion.2), channel_id=1, source_target_pairs={{0,1},{1,0},{2,3},{3,2},{4,5},{5,4},{6,7},{7,6},{8,9},{9,8},{10,11... | collective-permute-start | bytes 786440 | tf_op jit(solution)/shard_map/ppermute | solution.py:173
  112.0 3.6 %copy-start.8 = (bf16[2,4,128,128]{3,2,1,0:T(8,128)(2,1)}, bf16[2,4,128,128]{3,2,1,0:T(8,128)(2,1)S(1)}, u32[]{:S(2)}) copy-start(bf16[2,4,128,128]{3,2,1,0:T(8,128)(2,1)S(1)} %collective-permute-done.3.two) | copy-start | bytes 786436
  112.0 3.6 %copy-start.9 = (bf16[2,4,128,128]{3,2,1,0:T(8,128)(2,1)}, bf16[2,4,128,128]{3,2,1,0:T(8,128)(2,1)S(1)}, u32[]{:S(2)}) copy-start(bf16[2,4,128,128]{3,2,1,0:T(8,128)(2,1)S(1)} %collective-permute-done.4.swapped) | copy-start | bytes 786436
  115.6 0.8 copy-start.3
  123.5 19.6 %collective-permute-start.5 = (bf16[256,128]{1,0:T(8,128)(2,1)S(1)}, bf16[256,128]{1,0:T(8,128)(2,1)S(1)}, u32[]{:S(2)}, u32[]{:S(2)}) collective-permute-start(bf16[256,128]{1,0:T(8,128)(2,1)S(1)} %bitcast.56), channel_id=1, source_target_pairs={{0,0},{1,1},{2,32},{3,33},{4,64},{5,65},{6,96},{7,97},{8,128},{9,1... | collective-permute-start | bytes 196616 | tf_op jit(solution)/shard_map/ppermute | solution.py:185
